TPU v7x, 128 devices: a whole 4x4x4 slice. The times are simulated.
128 devices in a mesh: row: 8 (over x, z_lo), col: 16 (over y, z_hi, core).
Axes of the slice: x: 4, y: 4, z: 4 (z_hi: 2, z_lo: 2; z = z_hi * 2 + z_lo), core: 2. Of those that a mesh axis runs over, the one named last changes fastest.
Arguments:
- patch_rows: bfloat16 [131072, 1152], P(('row', 'col')), may hold values from -6 to 6
- segment_ids: int32 [128, 1024], P(('row', 'col')), may hold values from 0 to 7, never falling along the last dimension, each value on 1 to 256 neighbouring positions
- norm_gain: float32 [1152], replicated, may hold values from 0.25 to 1.75
- query_weight: bfloat16 [1152, 1152], P('col')
- key_weight: bfloat16 [1152, 1152], P('col')
- value_weight: bfloat16 [1152, 1152], P('col'), may hold values from -0.1875 to 0.1875
- out_weight: bfloat16 [1152, 1152], P('col'), may hold values from -0.1875 to 0.1875
- text_embeds: bfloat16 [1024, 1152], P(('row', 'col')), may hold values from -6 to 6
Outputs:
- encoded: bfloat16 [131072, 1152], P(('row', 'col'))
- image_grad: float32 [1024, 1152], P(('row', 'col'))
- text_grad: float32 [1024, 1152], P(('row', 'col'))
Inputs may be any that keep to these rules, and one draw needn't show every extreme that they name: `segment_ids`: within each packed sequence the image numbers never fall, every image 0 to 7 appears with 1 to 256 rows, and some image of every sequence has exactly 256 rows.
All inputs are finite; a program needn't handle non-finite values.
Results may differ from a plain program's by a relative error of at most 0.0095.
Values may be sent and summed in bfloat16 or wider, within the bound.
No kernel may reach another device: no remote copies, remote signals or barrier semaphores. Data moves between devices by JAX's collectives and lax.ppermute only.
A program may use at most 192 MiB of HBM per device.

v0:
```python
import jax
import jax.numpy as jnp
from jax import lax
from jax.sharding import PartitionSpec as P

HEADS = 16
IMG_DEV = 8


def add_rows(left, piece):
    return jnp.dot(left, piece, preferred_element_type=jnp.float32)


def unit_rows(values):
    return values * lax.rsqrt(jnp.sum(values * values, axis=1, keepdims=True) + 1e-06)


def body(
    patch_rows,
    segment_ids,
    norm_gain,
    query_weight,
    key_weight,
    value_weight,
    out_weight,
    text_embeds,
):
    count, width = patch_rows.shape
    head_dim = width // HEADS
    segs = segment_ids[0]
    xf = patch_rows.astype(jnp.float32)
    centre = xf - jnp.mean(xf, axis=1, keepdims=True)
    spread = jnp.mean(centre * centre, axis=1, keepdims=True)
    normed = (centre * lax.rsqrt(spread + 1e-06) * norm_gain).astype(jnp.bfloat16)

    def add_one(piece):
        return add_rows(normed, piece)

    queries = add_one(lax.all_gather(query_weight, "col", axis=0, tiled=True))
    keys = add_one(lax.all_gather(key_weight, "col", axis=0, tiled=True))
    values = add_one(lax.all_gather(value_weight, "col", axis=0, tiled=True))
    qh = queries.astype(jnp.bfloat16).reshape(count, HEADS, head_dim)
    kh = keys.astype(jnp.bfloat16).reshape(count, HEADS, head_dim)
    vh = values.astype(jnp.bfloat16).reshape(count, HEADS, head_dim)
    block = min(512, count)
    scale = 1.0 / jnp.sqrt(jnp.float32(head_dim))
    pieces = []
    for blk_index in range(count // block):
        low = blk_index * block
        q_block = qh[low : low + block]
        scores = jnp.einsum("qhd,khd->hqk", q_block, kh, preferred_element_type=jnp.float32) * scale
        same = segs[low : low + block][:, None] == segs[None, :]
        scores = jnp.where(same[None], scores, jnp.float32(-1e30))
        top = jnp.max(scores, axis=2, keepdims=True)
        expo = jnp.exp(scores - top)
        probs = (expo / jnp.sum(expo, axis=2, keepdims=True)).astype(jnp.bfloat16)
        context = jnp.einsum("hqk,khd->qhd", probs, vh, preferred_element_type=jnp.float32)
        pieces.append(context.astype(jnp.bfloat16).reshape(block, width))
    context = jnp.concatenate(pieces, axis=0)
    attended = add_rows(context, lax.all_gather(out_weight, "col", axis=0, tiled=True))
    encoded = (xf + attended).astype(jnp.bfloat16)
    onehot = (segs[None, :] == jnp.arange(IMG_DEV, dtype=jnp.int32)[:, None]).astype(jnp.bfloat16)
    sums = jnp.dot(onehot, encoded, preferred_element_type=jnp.float32)
    pooled = sums / jnp.sum(onehot.astype(jnp.float32), axis=1, keepdims=True)
    image_unit = unit_rows(pooled)
    text_unit = unit_rows(text_embeds.astype(jnp.float32))
    n_row = lax.axis_size("row")
    n_col = lax.axis_size("col")
    row_at = lax.axis_index("row")
    col_at = lax.axis_index("col")
    images = image_unit.shape[0]
    total_images = images * n_row * n_col
    every_text = lax.all_gather(text_unit, ("row", "col"), axis=0, tiled=True)
    own = (row_at * n_col + col_at) * images + jnp.arange(images, dtype=jnp.int32)
    text_ids = jnp.arange(total_images, dtype=jnp.int32)
    logits = 10.0 * jnp.dot(image_unit, every_text.T, precision=lax.Precision.HIGHEST) - 3.0
    sign = jnp.where(own[:, None] == text_ids[None, :], jnp.float32(1.0), jnp.float32(-1.0))
    coeffs = -sign * jax.nn.sigmoid(-sign * logits)
    image_grad = 10.0 * jnp.dot(coeffs, every_text, precision=lax.Precision.HIGHEST)
    text_grad = lax.psum_scatter(
        10.0 * jnp.dot(coeffs.T, image_unit, precision=lax.Precision.HIGHEST),
        ("row", "col"),
        scatter_dimension=0,
        tiled=True,
    )
    return (encoded, image_grad, text_grad)


def solution(mesh):
    return jax.shard_map(
        body,
        mesh=mesh,
        in_specs=(
            P(("row", "col"), None),
            P(("row", "col"), None),
            P(),
            P("col", None),
            P("col", None),
            P("col", None),
            P("col", None),
            P(("row", "col"), None),
        ),
        out_specs=(P(("row", "col"), None), P(("row", "col"), None), P(("row", "col"), None)),
        check_vma=False,
    )
```

profile of v0, /device:TPU:1, one launch (start us, length us, event | category | flops | bytes accessed | tf_op | source)
XLA Modules:
  0.0 594.1 jit_solution(13852529198441490243)
XLA Ops:
  10.9 1.4 convert_multiply_fusion
  12.4 2.0 convert_reduce_fusion
  15.9 1.6 broadcast_compare_fusion.1
  17.5 47.3 %all-gather.8.cloned.1.call-done = bf16[1152,1152]{1,0:T(8,128)(2,1)} async-done(((bf16[72,1152]{1,0:T(8,128)(2,1)}), bf16[1152,1152]{1,0:T(8,128)(2,1)}) %all-gather.8.cloned.1.call-update) | async-done | bytes 2654224 | tf_op jit(solution)/shard_map/all_gather | solution.py:39
  64.8 5.8 convolution_convert_fusion.1
  71.8 2.4 copy.26
  74.2 42.3 %all-gather.10.cloned.1.call-done = bf16[1152,1152]{1,0:T(8,128)(2,1)} async-done(((bf16[72,1152]{1,0:T(8,128)(2,1)}), bf16[1152,1152]{1,0:T(8,128)(2,1)}) %all-gather.10.cloned.1.call-update) | async-done | bytes 2654224 | tf_op jit(solution)/shard_map/all_gather | solution.py:40
  116.5 6.8 %convolution_convert_fusion = bf16[1024,1152]{1,0:T(8,128)(2,1)} fusion(bf16[1152,1152]{1,0:T(8,128)(2,1)} %all-gather.10.cloned.1.call-done, bf16[1024,1152]{1,0:T(8,128)(2,1)S(1)} %copy-done, f32[1152]{0:T(1024)} %param.10, f32[1024]{0:T(1024)S(1)} %add_rsqrt_fusion, f32[1024]{0:T(1024)S(1)} %broadcast_multiply_fusion), kind=kOutput, calls=%fused_computation.28 | convolution fusion | flops 2724986880 | bytes 7385600 | tf_op jit(solution)/shard_map/dot_general | solution.py:11
  123.3 4.3 copy.27
  127.6 1.4 copy.28
  129.0 17.9 %fusion.52 = (f32[16,512]{1,0:T(8,128)}, f32[16,512,1024]{2,1,0:T(8,128)}) fusion(pred[512,1024]{1,0:T(8,128)(4,1)} %get-tuple-element.5, bf16[512,16,72]{0,2,1:T(8,128)(2,1)} %bitcast.36, bf16[1024,16,72]{0,2,1:T(8,128)(2,1)} %bitcast.32), kind=kOutput, calls=%fused_computation.77 | convolution fusion | flops 1241515008 | bytes 37650432 | tf_op jit(solution)/shard_map/sub | solution.py:55
  147.0 17.8 %fusion.51 = (f32[16,512]{1,0:T(8,128)}, f32[16,512,1024]{2,1,0:T(8,128)}) fusion(pred[512,1024]{1,0:T(8,128)(4,1)} %get-tuple-element.6, bf16[512,16,72]{0,2,1:T(8,128)(2,1)S(1)} %bitcast.37, bf16[1024,16,72]{0,2,1:T(8,128)(2,1)} %bitcast.33), kind=kOutput, calls=%fused_computation.76 | convolution fusion | flops 1241515008 | bytes 37650432 | tf_op jit(solution)/shard_map/sub | solution.py:55
  164.8 3.5 all-gather.6.cloned.1.call-done
  168.3 6.8 %convolution_convert_fusion.2 = bf16[1024,1152]{1,0:T(8,128)(2,1)} fusion(bf16[1152,1152]{1,0:T(8,128)(2,1)} %all-gather.6.cloned.1.call-done, bf16[1024,1152]{1,0:T(8,128)(2,1)S(1)} %copy-done, f32[1152]{0:T(1024)} %param.10, f32[1024]{0:T(1024)S(1)} %add_rsqrt_fusion, f32[1024]{0:T(1024)S(1)} %broadcast_multiply_fusion), kind=kOutput, calls=%fused_computation.30 | convolution fusion | flops 2724986880 | bytes 7385600 | tf_op jit(solution)/shard_map/dot_general | solution.py:11
  175.1 4.3 copy.25
  179.4 14.1 %fusion.22 = bf16[16,72,512]{2,1,0:T(8,128)(2,1)S(1)} fusion(bf16[1024,16,72]{0,2,1:T(8,128)(2,1)} %bitcast.34, f32[16,512,1024]{2,1,0:T(8,128)} %get-tuple-element.12, f32[16,512]{1,0:T(8,128)} %get-tuple-element.11), kind=kOutput, calls=%fused_computation.37 | convolution fusion | flops 1225326592 | bytes 37126144 | tf_op jit(solution)/shard_map/hqk,khd->qhd/dot_general | solution.py:57
  193.5 15.4 %fusion.21 = bf16[16,72,512]{2,1,0:T(8,128)(2,1)} fusion(bf16[1024,16,72]{0,2,1:T(8,128)(2,1)} %bitcast.35, f32[16,512,1024]{2,1,0:T(8,128)} %get-tuple-element.10, f32[16,512]{1,0:T(8,128)} %get-tuple-element.9), kind=kOutput, calls=%fused_computation.36 | convolution fusion | flops 1225326592 | bytes 37126144 | tf_op jit(solution)/shard_map/hqk,khd->qhd/dot_general | solution.py:57
  208.9 11.0 %all-gather.12.cloned.1.call-done = bf16[1152,1152]{1,0:T(8,128)(2,1)} async-done(((bf16[72,1152]{1,0:T(8,128)(2,1)}), bf16[1152,1152]{1,0:T(8,128)(2,1)}) %all-gather.12.cloned.1.call-update) | async-done | bytes 2654224 | tf_op jit(solution)/shard_map/all_gather | solution.py:60
  219.9 5.7 fusion.17
  227.5 192.2 %all-gather.14.cloned.1.call-done = f32[1024,1152]{1,0:T(8,128)} async-done(((f32[8,1152]{1,0:T(8,128)}), f32[1024,1152]{1,0:T(8,128)}) %all-gather.14.cloned.1.call-update) | async-done | bytes 4718608 | tf_op jit(solution)/shard_map/all_gather | solution.py:73
  419.7 6.2 %fusion.29 = f32[8,1024]{1,0:T(8,128)S(1)} fusion(f32[1024,1152]{1,0:T(8,128)} %all-gather.14.cloned.1.call-done, f32[8,1152]{1,0:T(8,128)S(1)} %get-tuple-element.14, f32[8]{0:T(128)S(1)} %add_rsqrt_fusion.2, s32[8]{0:T(128)S(1)} %copy-done.4), kind=kOutput, calls=%fused_computation.45 | convolution fusion | flops 113337344 | bytes 4788288 | tf_op jit(solution)/shard_map/dot_general | solution.py:76
  425.9 5.7 convolution_multiply_fusion
  431.7 5.3 convolution_multiply_fusion.1
  436.9 149.0 %all-reduce.3.cloned.1.call-done = f32[1024,1152]{1,0:T(8,128)} async-done(((f32[1024,1152]{1,0:T(8,128)}), f32[1024,1152]{1,0:T(8,128)}) %all-reduce.3.cloned.1.call-update) | async-done | bytes 4718608
  (36 shorter events, 9.7 us)
Async XLA Ops:
  7.2 7.3 %copy-start = (bf16[1024,1152]{1,0:T(8,128)(2,1)S(1)}, bf16[1024,1152]{1,0:T(8,128)(2,1)}, u32[]{:S(2)}) copy-start(bf16[1024,1152]{1,0:T(8,128)(2,1)} %param.8) | copy-start | bytes 7077892
  7.2 57.6 %all-gather.8.cloned.1.call-start = ((), (), s32[]{:S(2)}) async-start(), calls=%async_computation.1 | async-start | bytes 2820096 | tf_op jit(solution)/shard_map/all_gather | solution.py:39
  7.9 7.3 %copy-start.3 = (s32[1,1024]{1,0:T(1,128)S(1)}, s32[1,1024]{1,0:T(1,128)}, u32[]{:S(2)}) copy-start(s32[1,1024]{1,0:T(1,128)} %param.9) | copy-start | bytes 12292
  7.9 108.6 %all-gather.10.cloned.1.call-start = ((), (), s32[]{:S(2)}) async-start(), calls=%async_computation.2 | async-start | bytes 2820096 | tf_op jit(solution)/shard_map/all_gather | solution.py:40
  8.7 159.6 %all-gather.6.cloned.1.call-start = ((), (), s32[]{:S(2)}) async-start(), calls=%async_computation | async-start | bytes 2820096 | tf_op jit(solution)/shard_map/all_gather | solution.py:41
  9.4 210.5 %all-gather.12.cloned.1.call-start = ((), (), s32[]{:S(2)}) async-start(), calls=%async_computation.3 | async-start | bytes 2820096 | tf_op jit(solution)/shard_map/all_gather | solution.py:60
  10.0 409.7 %all-gather.14.cloned.1.call-start = ((), (), s32[]{:S(2)}) async-start(), calls=%async_computation.4 | async-start | bytes 4755456 | tf_op jit(solution)/shard_map/all_gather | solution.py:73
  12.3 573.6 %all-reduce.3.cloned.1.call-start = ((), (), s32[]{:S(2)}) async-start(), calls=%async_computation.5 | async-start | bytes 9437184
  12.4 52.4 %copy-start.5 = (f32[1152]{0:T(1024)S(1)}, f32[1152]{0:T(1024)}, u32[]{:S(2)}) copy-start(f32[1152]{0:T(1024)} %param.10) | copy-start | bytes 13828
  129.0 17.9 %copy-start.2 = (bf16[512,1152]{0,1:T(8,128)(2,1)S(1)}, bf16[512,1152]{0,1:T(8,128)(2,1)}, u32[]{:S(2)}) copy-start(bf16[512,1152]{0,1:T(8,128)(2,1)} %copy.28) | copy-start | bytes 3538948
  219.9 199.8 %copy-start.4 = (s32[8]{0:T(128)S(1)}, s32[8]{0:T(128)}, u32[]{:S(2)}) copy-start(s32[8]{0:T(128)} %iota_add_fusion) | copy-start | bytes 100
  225.5 1.4 copy-start.1
Sparse Core Ops, SparseCore 0:
  10.5 54.2 all-gather.7
  67.3 49.1 all-gather.9
  119.1 49.1 all-gather.5
  170.7 49.1 all-gather.11
  222.0 197.6 all-gather.13
  431.8 154.0 all-reduce.2
where the time goes:
time: 595 us; the launch traced here: 594 us
  waiting for transfers between devices  448 us (75%)
  matrix products  108 us (18%)
  local copies, waits for them, and re-layouts  16.5 us (3%)
  between operations  14.2 us (2%)
  other arithmetic  7.37 us (1%)
    all_gather x1, waiting for transfers between devices, body(): every_text = lax.all_gather(text_unit, ('row', 'col'), axis=0, tiled=True)  192 us
    unnamed x7, waiting for transfers between devices  152 us
    all_gather x1, waiting for transfers between devices, body(): queries = add_one(lax.all_gather(query_weight, 'col', axis=0, tiled=True))  47.3 us
    all_gather x1, waiting for transfers between devices, body(): keys = add_one(lax.all_gather(key_weight, 'col', axis=0, tiled=True))  42.3 us
    sub x2, matrix products, body(): expo = jnp.exp(scores - top)  35.7 us
    dot_general x2, matrix products, body(): jnp.einsum('hqk,khd->qhd', probs, vh, preferred_element_type=jnp.float32)  29.5 us
    dot_general x4, matrix products, add_rows(): return jnp.dot(left, piece, preferred_element_type=jnp.float32)  25 us
  transfers between devices with their start and end apart: 6, of which 6 were waited for; matrix products, arithmetic and copies ran while one was open for 20% of the time, Pallas kernels for 0%

commit v1 on v0

v1 whole, which is shorter than its diff:
```python
import math

import jax
import jax.numpy as jnp
from jax import lax
from jax.experimental import pallas as pl
from jax.experimental.pallas import tpu as pltpu
from jax.sharding import PartitionSpec as P

HEADS = 16
IMG_DEV = 8
MASKED = -1e30
QUERY_ROWS = 256
KEY_ROWS = 128
F32 = jnp.float32
BF16 = jnp.bfloat16
VMEM = pl.BlockSpec(memory_space=pltpu.VMEM)
SMEM = pl.BlockSpec(memory_space=pltpu.SMEM)
BIG = pltpu.CompilerParams(vmem_limit_bytes=58 * 2**20)


def norm_kernel(x_ref, gain_ref, seg_ref, normed_ref, query_mark_ref, key_mark_ref):
    count = x_ref.shape[0]

    def one(i, _):
        rows = pl.ds(pl.multiple_of(i * 128, 128), 128)
        xf = x_ref[rows, :].astype(F32)
        centre = xf - jnp.mean(xf, axis=1, keepdims=True)
        spread = jnp.mean(centre * centre, axis=1, keepdims=True)
        normed_ref[rows, :] = (centre * lax.rsqrt(spread + 1e-06) * gain_ref[...]).astype(BF16)
        mine = seg_ref[rows, :] == lax.broadcasted_iota(jnp.int32, (128, 256), 1) % IMG_DEV
        query_mark_ref[rows, :] = jnp.where(mine, 1.0, 0.0).astype(BF16)
        key_mark_ref[rows, :] = jnp.where(mine, 0.0, MASKED).astype(BF16)
        return 0

    lax.fori_loop(0, count // 128, one, 0)


def norm(x, gain, segs):
    count, width = x.shape
    return pl.pallas_call(
        norm_kernel,
        out_shape=(
            jax.ShapeDtypeStruct((count, width), BF16),
            jax.ShapeDtypeStruct((count, 256), BF16),
            jax.ShapeDtypeStruct((count, 256), BF16),
        ),
        in_specs=[VMEM] * 3,
        out_specs=(VMEM,) * 3,
        compiler_params=BIG,
        name="norm",
    )(x, gain.reshape(1, width), segs.reshape(count, 1))


def attend_kernel(
    x_ref, normed_ref, query_mark_ref, key_mark_ref, segs_ref, window_ref, weight_ref,
    context_ref, rows_sum_ref, context_sum_ref, q_s, k_s, v_s,
):
    count, width = normed_ref.shape
    head_dim = width // HEADS
    scale = math.log2(math.e) / math.sqrt(head_dim)

    def project(i, _):
        rows = pl.ds(pl.multiple_of(i * 256, 256), 256)
        normed = normed_ref[rows, :]

        def one(at):
            return jnp.dot(normed, weight_ref[:, at * width : (at + 1) * width], preferred_element_type=F32)

        q_s[rows, :] = (one(0) * scale).astype(BF16)
        k_s[rows, :] = one(1).astype(BF16)
        v_s[rows, :] = one(2).astype(BF16)
        return 0

    lax.fori_loop(0, count // 256, project, 0)
    lane = lax.broadcasted_iota(jnp.int32, (1, 256), 1)

    def block(at, blocks, first):
        qr = pl.ds(pl.multiple_of(at * QUERY_ROWS, QUERY_ROWS), QUERY_ROWS)
        kr = pl.ds(pl.multiple_of(first * KEY_ROWS, KEY_ROWS), blocks * KEY_ROWS)
        query_mark = query_mark_ref[qr, :]
        key_mark = key_mark_ref[kr, :]
        for head in range(HEADS):
            low = head * head_dim
            base = low // 128 * 128
            wide = 128 if low + head_dim <= base + 128 else 256
            mine = (lane[:, :wide] >= low - base) & (lane[:, :wide] < low - base + head_dim)
            cols = slice(base, base + wide)
            queries = jnp.where(mine, q_s[qr, cols], query_mark[:, :wide])
            keys = jnp.where(mine, k_s[kr, cols], key_mark[:, :wide])
            values = jnp.where(mine, v_s[kr, cols], jnp.ones((), BF16))
            scores = lax.dot_general(queries, keys, (((1,), (1,)), ((), ())), preferred_element_type=F32)
            top = jnp.max(scores, axis=1, keepdims=True)
            probs = jnp.exp2(scores - top).astype(BF16)
            out = jnp.dot(probs, values, preferred_element_type=F32)
            spare = 0 if low > base else wide - 1
            out = (out * (1.0 / out[:, spare : spare + 1])).astype(BF16)
            if low > base:
                out = jnp.where(mine, out, context_ref[qr, cols])
            context_ref[qr, cols] = out

    def one_block(at, _):
        first = window_ref[0, at]
        blocks = window_ref[1, at]
        for size in (3, 4, 5, 6):

            @pl.when((blocks == size) if size > 3 else (blocks <= 3))
            def _():
                block(at, size, jnp.minimum(first, count // KEY_ROWS - size))

        return 0

    lax.fori_loop(0, count // QUERY_ROWS, one_block, 0)
    member = (segs_ref[...] == lax.broadcasted_iota(jnp.int32, (IMG_DEV, count), 0)).astype(F32)
    member = member.astype(BF16)
    total = jnp.sum(member.astype(F32), axis=1, keepdims=True)
    rows_sum_ref[...] = jnp.dot(member, x_ref[...], preferred_element_type=F32) / total
    context_sum_ref[...] = jnp.dot(member, context_ref[...], preferred_element_type=F32) / total


def key_windows(segs):
    blocks = segs.reshape(-1, QUERY_ROWS)
    start = jnp.sum((segs[None, :] < blocks[:, :1]).astype(jnp.int32), axis=1)
    end = jnp.sum((segs[None, :] <= blocks[:, -1:]).astype(jnp.int32), axis=1)
    first = start // KEY_ROWS
    return jnp.stack([first, (end + KEY_ROWS - 1) // KEY_ROWS - first])


def attend(x, normed, query_mark, key_mark, segs, weights):
    count, width = x.shape
    small = jax.ShapeDtypeStruct((IMG_DEV, width), F32)
    return pl.pallas_call(
        attend_kernel,
        grid=(1,),
        out_shape=(jax.ShapeDtypeStruct((count, width), BF16), small, small),
        in_specs=[VMEM] * 5 + [SMEM, pl.BlockSpec((width, 3 * width), lambda i: (0, 0), pipeline_mode=pl.Buffered(1))],
        out_specs=(VMEM,) * 3,
        scratch_shapes=[pltpu.VMEM((count, width), BF16)] * 3,
        compiler_params=BIG,
        name="attend",
    )(x, normed, query_mark, key_mark, segs.reshape(1, count), key_windows(segs), weights)


def split(values):
    high = values.astype(BF16)
    return jnp.concatenate([high, (values - high.astype(F32)).astype(BF16)], axis=0)


def join(values):
    half = values.shape[0] // 2
    return values[:half] + values[half:]


def pool_kernel(rows_mean_ref, context_mean_ref, weight_ref, unit_ref, short_ref):
    pooled = rows_mean_ref[...] + join(jnp.dot(split(context_mean_ref[...]), weight_ref[...], preferred_element_type=F32))
    unit = pooled * lax.rsqrt(jnp.sum(pooled * pooled, axis=1, keepdims=True) + 1e-06)
    unit_ref[...] = unit
    short_ref[...] = unit.astype(BF16)


def pool(rows_mean, context_mean, weights):
    images, width = rows_mean.shape
    return pl.pallas_call(
        pool_kernel,
        grid=(1,),
        out_shape=(jax.ShapeDtypeStruct((images, width), F32), jax.ShapeDtypeStruct((images, width), BF16)),
        in_specs=[VMEM] * 2 + [pl.BlockSpec((width, width), lambda i: (0, 3))],
        out_specs=(VMEM,) * 2,
        compiler_params=BIG,
        name="pool",
    )(rows_mean, context_mean, weights)


def encode_kernel(x_ref, context_ref, weight_ref, out_ref):
    attended = jnp.dot(context_ref[...], weight_ref[...], preferred_element_type=F32)
    out_ref[...] = (x_ref[...].astype(F32) + attended).astype(BF16)


def encode(x, context, weights):
    count, width = x.shape
    rows = 256
    block = pl.BlockSpec((rows, width), lambda i: (i, 0))
    return pl.pallas_call(
        encode_kernel,
        grid=(count // rows,),
        out_shape=jax.ShapeDtypeStruct((count, width), BF16),
        in_specs=[block, block, pl.BlockSpec((width, width), lambda i: (0, 3))],
        out_specs=block,
        compiler_params=BIG,
        name="encode",
    )(x, context, weights)


def sigmoid_coeffs(logits, diagonal):
    sign = jnp.where(diagonal, 1.0, -1.0).astype(F32)
    return -sign * jax.nn.sigmoid(-sign * logits)


def image_kernel(place_ref, unit_ref, text_ref, scale_ref, out_ref):
    images = unit_ref.shape[0]
    count = text_ref.shape[0]
    text = text_ref[...]
    scale = scale_ref[...]
    dots = lax.dot_general(split(unit_ref[...]), text, (((1,), (1,)), ((), ())), preferred_element_type=F32)
    logits = 10.0 * join(dots) * scale - 3.0
    own = place_ref[0] * images + lax.broadcasted_iota(jnp.int32, (images, count), 0)
    coeffs = sigmoid_coeffs(logits, own == lax.broadcasted_iota(jnp.int32, (images, count), 1))
    out_ref[...] = 10.0 * join(jnp.dot(split(coeffs * scale), text, preferred_element_type=F32))


def image_gradient(place, unit, text, scale):
    return pl.pallas_call(
        image_kernel,
        out_shape=jax.ShapeDtypeStruct(unit.shape, F32),
        in_specs=[SMEM] + [VMEM] * 3,
        out_specs=VMEM,
        compiler_params=BIG,
        name="image_gradient",
    )(place, unit, text, scale)


def text_kernel(place_ref, units_ref, text_ref, out_ref):
    images = units_ref.shape[0]
    count = text_ref.shape[0]
    text = text_ref[...].astype(F32)
    text = text * lax.rsqrt(jnp.sum(text * text, axis=1, keepdims=True) + 1e-06)
    units = units_ref[...]
    dots = lax.dot_general(split(text), units, (((1,), (1,)), ((), ())), preferred_element_type=F32)
    logits = 10.0 * join(dots) - 3.0
    image = lax.broadcasted_iota(jnp.int32, (count, images), 1) - place_ref[1] * IMG_DEV
    index = lax.broadcasted_iota(jnp.int32, (count, images), 0) - place_ref[2] * IMG_DEV
    coeffs = sigmoid_coeffs(logits, (image == index) & (image >= 0) & (image < IMG_DEV))
    out_ref[...] = 10.0 * join(jnp.dot(split(coeffs), units, preferred_element_type=F32))


def text_gradient(place, units, text):
    return pl.pallas_call(
        text_kernel,
        out_shape=jax.ShapeDtypeStruct(text.shape, F32),
        in_specs=[SMEM] + [VMEM] * 2,
        out_specs=VMEM,
        compiler_params=BIG,
        name="text_gradient",
    )(place, units, text)


def body(
    patch_rows,
    segment_ids,
    norm_gain,
    query_weight,
    key_weight,
    value_weight,
    out_weight,
    text_embeds,
):
    count, width = patch_rows.shape
    segs = segment_ids[0]
    n_row = lax.axis_size("row")
    n_col = lax.axis_size("col")
    row_at = lax.axis_index("row")
    col_at = lax.axis_index("col")
    place = jnp.stack([row_at * n_col + col_at, row_at, col_at]).astype(jnp.int32)
    depth = query_weight.shape[0]
    texts = text_embeds.shape[0]
    lanes = texts * width // depth
    packed = jnp.concatenate(
        [query_weight, key_weight, value_weight, out_weight, text_embeds.reshape(depth, lanes)], axis=1
    )
    weights = lax.all_gather(packed, "col", axis=0, tiled=True)
    row_text = weights[:, 4 * width :].reshape(n_col * texts, width)
    text = lax.all_gather(row_text, "row", axis=0, tiled=True)
    textf = text.astype(F32)
    text_scale = lax.rsqrt(jnp.sum(textf * textf, axis=1) + 1e-06).reshape(1, -1)
    normed, query_mark, key_mark = norm(patch_rows, norm_gain, segs)
    context, rows_mean, context_mean = attend(patch_rows, normed, query_mark, key_mark, segs, weights)
    unit, short = pool(rows_mean, context_mean, weights)
    units = lax.all_to_all(jnp.broadcast_to(short[None], (n_row,) + short.shape), "row", 0, 0)
    encoded = encode(patch_rows, context, weights)
    image_grad = image_gradient(place, unit, text, text_scale)
    partial = text_gradient(place, units.reshape(n_row * IMG_DEV, width), row_text)
    partial = lax.all_to_all(partial.reshape(n_col, texts, width), "col", 0, 0)
    text_grad = jnp.sum(partial, axis=0)
    return (encoded, image_grad, text_grad)


def solution(mesh):
    return jax.shard_map(
        body,
        mesh=mesh,
        in_specs=(
            P(("row", "col"), None),
            P(("row", "col"), None),
            P(),
            P("col", None),
            P("col", None),
            P("col", None),
            P("col", None),
            P(("row", "col"), None),
        ),
        out_specs=(P(("row", "col"), None), P(("row", "col"), None), P(("row", "col"), None)),
        check_vma=False,
    )
```

time: 595 us -> 195 us (0.33)
  waiting for transfers between devices: 448 us -> 96 us
  matrix products: 108 us -> 0 us
  Pallas kernels: 0 us -> 56.5 us
  starting transfers between devices: 0.23 us -> 11.1 us
    all_gather x5 -> x2, waiting for transfers between devices: 296 us -> 87.1 us  [the longest x1 87.1 us: body(): weights = lax.all_gather(packed, 'col', axis=0, tiled=True)]
    unnamed x7 -> x2, waiting for transfers between devices: 152 us -> 0.03 us
    dot_general x10 -> x0, matrix products: 72.3 us -> none  [the longest x2 29.5 us: body(): jnp.einsum('hqk,khd->qhd', probs, vh, preferred_element_type=jnp.float32)]
    pallas_call x0 -> x6, Pallas kernels: none -> 56.5 us  [the longest x1 34.1 us: attend(): pl.pallas_call(attend_kernel, grid=(1,), out_shape=(jax.ShapeDtypeStruct(...]
    sub x2 -> x0, matrix products: 35.7 us -> none  [body(): expo = jnp.exp(scores - top)]
    all_to_all x0 -> x2, starting transfers between devices: none -> 11.1 us  [the longest x1 7.02 us: body(): partial = lax.all_to_all(partial.reshape(n_col, texts, width), 'col', 0, 0)]
    all_to_all x0 -> x2, waiting for transfers between devices: none -> 8.87 us  [the longest x1 4.73 us: body(): lax.all_to_all(jnp.broadcast_to(short[None], (n_row,) + short.shape), 'ro...]
    convert_element_type x2 -> x0, local copies, waits for them, and re-layouts: 8.6 us -> none  [the longest x1 4.31 us: body(): vh = values.astype(jnp.bfloat16).reshape(count, HEADS, head_dim)]
  transfers between devices with their start and end apart: 6 -> 4, of which waited for: 6 -> 3; matrix products, arithmetic and copies ran while one was open for 20% -> 3% of each run, Pallas kernels for 0% -> 27%
where the time goes in v1:
time: 195 us
  waiting for transfers between devices  96 us (49%)
  Pallas kernels  56.5 us (29%)
  between operations  14.1 us (7%)
  local copies, waits for them, and re-layouts  11.9 us (6%)
  starting transfers between devices  11.1 us (6%)
  other arithmetic  5.51 us (3%)
    all_gather x1, waiting for transfers between devices, body(): weights = lax.all_gather(packed, 'col', axis=0, tiled=True)  87.1 us
    pallas_call x1, Pallas kernels, attend(): pl.pallas_call(attend_kernel, grid=(1,), out_shape=(jax.ShapeDtypeStruct(...  34.1 us
    pallas_call x1, Pallas kernels, encode(): pl.pallas_call(encode_kernel, grid=(count // rows,), out_shape=jax.ShapeD...  7.52 us
    all_to_all x1, starting transfers between devices, body(): partial = lax.all_to_all(partial.reshape(n_col, texts, width), 'col', 0, 0)  7.02 us
    unnamed x15, local copies, waits for them, and re-layouts  5.95 us
    pallas_call x1, Pallas kernels, norm(): pl.pallas_call(norm_kernel, out_shape=(jax.ShapeDtypeStruct((count, width...  5.8 us
    all_to_all x1, waiting for transfers between devices, body(): lax.all_to_all(jnp.broadcast_to(short[None], (n_row,) + short.shape), 'ro...  4.73 us
    all_to_all x1, waiting for transfers between devices, body(): partial = lax.all_to_all(partial.reshape(n_col, texts, width), 'col', 0, 0)  4.14 us
  transfers between devices with their start and end apart: 4, of which 3 were waited for; matrix products, arithmetic and copies ran while one was open for 3% of the time, Pallas kernels for 27%

profile of v1, /device:TPU:1, one launch (start us, length us, event | category | flops | bytes accessed | tf_op | source)
XLA Modules:
  0.0 195.1 jit_solution(10222414328357819950)
XLA Ops:
  7.2 0.9 constant_dynamic-update-slice_fusion.4
  8.2 0.8 reshape.147
  8.9 0.9 constant_dynamic-update-slice_fusion.3
  9.9 0.9 constant_dynamic-update-slice_fusion.2
  10.8 0.9 constant_dynamic-update-slice_fusion.1
  11.8 0.8 copy-done
  12.7 87.1 %all-gather.3.cloned.1.call-done.weight_ref = bf16[1152,4736]{1,0:T(8,128)(2,1)} async-done(((bf16[72,4736]{1,0:T(8,128)(2,1)}), bf16[1152,4736]{1,0:T(8,128)(2,1)}) %all-gather.3.cloned.1.call-update) | async-done | bytes 10911760 | tf_op jit(solution)/shard_map/all_gather | solution.py:270
  99.8 1.0 slice.14
  100.8 1.1 reshape.148.text_ref
  102.4 0.7 reduce.3
  103.3 1.0 copy.16.seg_ref
  105.0 5.8 %norm.1 = (bf16[1024,1152]{1,0:T(8,128)(2,1)}, bf16[1024,256]{1,0:T(8,128)(2,1)}, bf16[1024,256]{1,0:T(8,128)(2,1)}) custom-call(bf16[1024,1152]{1,0:T(8,128)(2,1)} %x_ref.5, f32[1,1152]{1,0:T(1,128)} %reshape.146.gain_ref, s32[1024,1]{1,0:T(8,128)} %copy.16.seg_ref), custom_call_target="tpu_custom_call" | custom-call | tf_op jit(solution)/shard_map/norm/pallas_call | solution.py:41
  111.6 34.1 %attend.1 = (bf16[1024,1152]{1,0:T(8,128)(2,1)}, f32[8,1152]{1,0:T(8,128)}, f32[8,1152]{1,0:T(8,128)}) custom-call(bf16[1024,1152]{1,0:T(8,128)(2,1)} %x_ref.5, bf16[1024,1152]{1,0:T(8,128)(2,1)} %get-tuple-element.11.normed_ref, bf16[1024,256]{1,0:T(8,128)(2,1)} %get-tuple-element.12.query_mark_ref, bf16[1024,256]{1,0:T(8,128)(2,1)} %get-tuple-element.13.key_mark_ref, ...), custom_call_target="tpu_custom_call" | custom-call | tf_op jit(solution)/shard_map/attend/pallas_call | solution.py:132
  145.7 3.0 %pool.1 = (f32[8,1152]{1,0:T(8,128)}, bf16[8,1152]{1,0:T(8,128)(2,1)}) custom-call(f32[8,1152]{1,0:T(8,128)} %get-tuple-element.15.rows_mean_ref, f32[8,1152]{1,0:T(8,128)} %get-tuple-element.16.context_mean_ref, bf16[1152,4736]{1,0:T(8,128)(2,1)} %all-gather.3.cloned.1.call-done.weight_ref), custom_call_target="tpu_custom_call" | custom-call | tf_op jit(solution)/shard_map/pool/pallas_call | solution.py:163
  148.6 1.4 broadcast_in_dim.2
  150.0 4.0 %all-to-all-start = ((bf16[8,8,1152]{2,1,0:T(8,128)(2,1)}), bf16[8,8,1152]{2,1,0:T(8,128)(2,1)S(1)}, u32[]{:S(2)}, u32[]{:S(2)}) async-start(bf16[8,8,1152]{2,1,0:T(8,128)(2,1)} %broadcast_in_dim.2), calls=%async_computation | async-start | bytes 294912 | tf_op jit(solution)/shard_map/all_to_all | solution.py:278
  154.7 4.7 %all-to-all-done = bf16[8,8,1152]{2,1,0:T(8,128)(2,1)S(1)} async-done(((bf16[8,8,1152]{2,1,0:T(8,128)(2,1)}), bf16[8,8,1152]{2,1,0:T(8,128)(2,1)S(1)}, u32[]{:S(2)}, u32[]{:S(2)}) %all-to-all-start) | async-done | bytes 147488 | tf_op jit(solution)/shard_map/all_to_all | solution.py:278
  159.4 0.7 copy-done.1
  160.1 2.8 %text_gradient.1 = f32[128,1152]{1,0:T(8,128)} custom-call(s32[3]{0:T(128)} %pad_add_fusion.1.place_ref, bf16[64,1152]{1,0:T(8,128)(2,1)} %bitcast.31, bf16[128,1152]{1,0:T(8,128)(2,1)} %reshape.148.text_ref), custom_call_target="tpu_custom_call" | custom-call | tf_op jit(solution)/shard_map/text_gradient/pallas_call | solution.py:237
  162.8 7.0 %all-to-all-start.1 = ((f32[16,8,1152]{2,1,0:T(8,128)}), f32[16,8,1152]{2,1,0:T(8,128)S(1)}, u32[]{:S(2)}, u32[]{:S(2)}) async-start(f32[16,8,1152]{2,1,0:T(8,128)} %bitcast.30), calls=%async_computation.1 | async-start | bytes 1179648 | tf_op jit(solution)/shard_map/all_to_all | solution.py:282
  169.8 7.5 %encode.1 = bf16[1024,1152]{1,0:T(8,128)(2,1)} custom-call(bf16[1024,1152]{1,0:T(8,128)(2,1)} %x_ref.5, bf16[1024,1152]{1,0:T(8,128)(2,1)} %get-tuple-element.14.context_ref, bf16[1152,4736]{1,0:T(8,128)(2,1)} %all-gather.3.cloned.1.call-done.weight_ref), custom_call_target="tpu_custom_call" | custom-call | tf_op jit(solution)/shard_map/encode/pallas_call | solution.py:183
  177.4 4.1 %all-to-all-done.1 = f32[16,8,1152]{2,1,0:T(8,128)S(1)} async-done(((f32[16,8,1152]{2,1,0:T(8,128)}), f32[16,8,1152]{2,1,0:T(8,128)S(1)}, u32[]{:S(2)}, u32[]{:S(2)}) %all-to-all-start.1) | async-done | bytes 589856 | tf_op jit(solution)/shard_map/all_to_all | solution.py:282
  182.1 2.2 %multiply_reduce_fusion = f32[1024]{0:T(1024)S(1)} fusion(bf16[1024,1152]{1,0:T(8,128)(2,1)} %all-gather.5.cloned.1.call-done.text_ref), kind=kLoop, calls=%fused_computation | loop fusion | flops 3537920 | bytes 2363392 | tf_op jit(solution)/shard_map/reduce_sum | solution.py:274
  184.9 3.4 %image_gradient.1 = f32[8,1152]{1,0:T(8,128)} custom-call(s32[3]{0:T(128)} %pad_add_fusion.1.place_ref, f32[8,1152]{1,0:T(8,128)} %get-tuple-element.17.unit_ref, bf16[1024,1152]{1,0:T(8,128)(2,1)} %all-gather.5.cloned.1.call-done.text_ref, f32[1,1024]{1,0:T(1,128)} %bitcast.34), custom_call_target="tpu_custom_call" | custom-call | tf_op jit(solution)/shard_map/image_gradient/pallas_call | solution.py:212
  (24 shorter events, 4.2 us)
Async XLA Ops:
  7.2 95.2 %copy-start.2 = (s32[1,1024]{1,0:T(1,128)S(1)}, s32[1,1024]{1,0:T(1,128)}, u32[]{:S(2)}) copy-start(s32[1,1024]{1,0:T(1,128)} %segs_ref.1) | copy-start | bytes 12292
  7.2 97.2 %copy-start.3 = (f32[1152]{0:T(1024)S(1)}, f32[1152]{0:T(1024)}, u32[]{:S(2)}) copy-start(f32[1152]{0:T(1024)} %param.10) | copy-start | bytes 13828
  7.2 92.6 %all-gather.3.cloned.1.call-start = ((), (), s32[]{:S(2)}) async-start(), calls=%async_computation.2 | async-start | bytes 11593728 | tf_op jit(solution)/shard_map/all_gather | solution.py:270
  11.8 0.8 copy-start
  12.6 169.5 %all-gather.5.cloned.1.call-start = ((), (), s32[]{:S(2)}) async-start(), calls=%async_computation.3 | async-start | bytes 2654208 | tf_op jit(solution)/shard_map/all_gather | solution.py:272
  150.0 9.4 %all-to-all-start = ((bf16[8,8,1152]{2,1,0:T(8,128)(2,1)}), bf16[8,8,1152]{2,1,0:T(8,128)(2,1)S(1)}, u32[]{:S(2)}, u32[]{:S(2)}) async-start(bf16[8,8,1152]{2,1,0:T(8,128)(2,1)} %broadcast_in_dim.2), calls=%async_computation | async-start | bytes 294912 | tf_op jit(solution)/shard_map/all_to_all | solution.py:278
  159.4 0.7 copy-start.1
  162.8 18.7 %all-to-all-start.1 = ((f32[16,8,1152]{2,1,0:T(8,128)}), f32[16,8,1152]{2,1,0:T(8,128)S(1)}, u32[]{:S(2)}, u32[]{:S(2)}) async-start(f32[16,8,1152]{2,1,0:T(8,128)} %bitcast.30), calls=%async_computation.1 | async-start | bytes 1179648 | tf_op jit(solution)/shard_map/all_to_all | solution.py:282
Sparse Core Ops, SparseCore 0:
  12.8 86.9 all-gather.2
  102.0 52.0 all-gather.4

commit v2 on v0

v2 whole, which is shorter than its diff:
```python
import math

import jax
import jax.numpy as jnp
from jax import lax
from jax.experimental import pallas as pl
from jax.experimental.pallas import tpu as pltpu
from jax.sharding import PartitionSpec as P

HEADS = 16
IMG_DEV = 8
MASKED = -1e30
QUERY_ROWS = 256
KEY_ROWS = 128
SIDE = 4
AXES = ("row", "col")
F32 = jnp.float32
BF16 = jnp.bfloat16
VMEM = pl.BlockSpec(memory_space=pltpu.VMEM)
SMEM = pl.BlockSpec(memory_space=pltpu.SMEM)
ANY = pl.BlockSpec(memory_space=pl.ANY)


def whole(shape):
    return pl.BlockSpec(shape, lambda i: (0,) * len(shape), pipeline_mode=pl.Buffered(1))


def params():
    return pltpu.CompilerParams(vmem_limit_bytes=60 * 2**20)


def cost(flops, bytes_accessed):
    return pl.CostEstimate(flops=flops, bytes_accessed=bytes_accessed, transcendentals=0)


def pairs(source_of):
    def flat(x, y, z, core):
        x, y, z = x % SIDE, y % SIDE, z % SIDE
        return (x * 2 + z % 2) * 16 + y * 4 + z // 2 * 2 + core

    found = []
    for x in range(SIDE):
        for y in range(SIDE):
            for z in range(SIDE):
                for core in range(2):
                    found.append((flat(*source_of(x, y, z, core)), flat(x, y, z, core)))
    return found


FROM_CORE = pairs(lambda x, y, z, core: (x, y, z, 1 - core))
FROM_UP = pairs(lambda x, y, z, core: (x, y + 1, z, core))
FROM_DOWN = pairs(lambda x, y, z, core: (x, y - 1, z, core))
FROM_ACROSS = pairs(lambda x, y, z, core: (x, y, 3 - z, core))


def take(values, found):
    return lax.ppermute(values, AXES, found)


def pack_kernel(place_ref, q_ref, k_ref, v_ref, o_ref, text_ref, mine_ref, other_ref, rest_ref, copies_ref):
    width = q_ref.shape[1]
    half = width // 2

    def columns(at):
        cols = slice(at * half, (at + 1) * half)
        return jnp.concatenate([q_ref[:, cols], v_ref[:, cols], k_ref[:, cols]], axis=1)

    first, second = columns(0), columns(1)
    core = jnp.full(first.shape, place_ref[3], jnp.int32) == 0
    mine_ref[...] = jnp.where(core, first.astype(F32), second.astype(F32)).astype(BF16)
    other_ref[...] = jnp.where(core, second.astype(F32), first.astype(F32)).astype(BF16)
    rest_ref[:, :width] = o_ref[...]
    text = text_ref[...].astype(F32)
    blocks = [text[:, at : at + 128] for at in range(0, width, 128)]
    rest_ref[:, width:] = jnp.concatenate(blocks, axis=0).astype(BF16)
    copies_ref[...] = jnp.broadcast_to(text_ref[...][None], copies_ref.shape)


def pack(place, q, k, v, o, text, copies):
    depth, width = q.shape
    part = (depth, width // 2 * 3)
    outs = (part, part, (depth, width + 128), (copies,) + text.shape)
    return pl.pallas_call(
        pack_kernel,
        grid=(1,),
        out_shape=tuple(jax.ShapeDtypeStruct(out, BF16) for out in outs),
        in_specs=[SMEM] + [whole(values.shape) for values in (q, k, v, o, text)],
        out_specs=tuple(whole(out) for out in outs),
        compiler_params=params(),
        cost_estimate=cost(0, 2**21),
        name="pack",
    )(place, q, k, v, o, text)


def norm_kernel(x_ref, gain_ref, segs_ref, out_ref, mean_ref):
    count, width = x_ref.shape
    segs = segs_ref[...]
    marks = (segs == lax.broadcasted_iota(jnp.int32, (128, count), 0) % IMG_DEV).astype(F32)
    out_ref[:, width:] = marks.T.astype(BF16)

    def one(i, _):
        rows = pl.ds(pl.multiple_of(i * 128, 128), 128)
        xf = x_ref[rows, :].astype(F32)
        centre = xf - jnp.mean(xf, axis=1, keepdims=True)
        spread = jnp.mean(centre * centre, axis=1, keepdims=True)
        out_ref[rows, :width] = (centre * lax.rsqrt(spread + 1e-06) * gain_ref[...]).astype(BF16)
        return 0

    lax.fori_loop(0, count // 128, one, 0)
    member = marks[:IMG_DEV]
    total = jnp.sum(member, axis=1, keepdims=True)
    mean_ref[...] = jnp.dot(member.astype(BF16), x_ref[...], preferred_element_type=F32) / total


def norm(x, gain, segs):
    count, width = x.shape
    return pl.pallas_call(
        norm_kernel,
        grid=(1,),
        out_shape=(
            jax.ShapeDtypeStruct((count, width + 128), BF16),
            jax.ShapeDtypeStruct((IMG_DEV, width), F32),
        ),
        in_specs=[whole(x.shape), whole((1, width)), whole(segs.shape)],
        out_specs=(whole((count, width + 128)), whole((IMG_DEV, width))),
        compiler_params=params(),
        cost_estimate=cost(0, 2**24),
        name="norm",
    )(x, gain.reshape(1, width), segs)


def split(values):
    high = values.astype(BF16)
    return jnp.concatenate([high, (values - high.astype(F32)).astype(BF16)], axis=0)


def join(values):
    half = values.shape[0] // 2
    return values[:half] + values[half:]


def attend_kernel(place_ref, window_ref, segs_ref, normed_hbm, *refs):
    shards, (context_ref, normed_ref, weight_s, qvk_s, sems) = refs[:-5], refs[-5:]
    count = normed_ref.shape[0]
    width = weight_s.shape[0]
    half = width // 2
    head_dim = width // HEADS
    shift = half // 128 * 128

    copies = [pltpu.make_async_copy(normed_hbm, normed_ref, sems.at[len(shards)])]
    for at, shard in enumerate(shards):
        whole = min(at, 7)
        row = place_ref[4 + whole]
        if at >= 7:
            row = row + (at - 7) * shard.shape[0]
        rows = pl.ds(pl.multiple_of(row, 16), shard.shape[0])
        copies.append(pltpu.make_async_copy(shard, weight_s.at[rows, :], sems.at[at]))
    for copy in copies:
        copy.start()
    for copy in copies:
        copy.wait()

    lanes = lax.broadcasted_iota(jnp.int32, (1, 3 * half), 1)
    scale = jnp.where(lanes < half, math.log2(math.e) / math.sqrt(head_dim), 1.0).astype(F32)

    def project(i, _):
        rows = pl.ds(pl.multiple_of(i * 256, 256), 256)
        out = jnp.dot(normed_ref[rows, :width], weight_s[...], preferred_element_type=F32)
        qvk_s[rows, : 3 * half] = (out * scale).astype(BF16)
        return 0

    lax.fori_loop(0, count // 256, project, 0)
    lane = lax.broadcasted_iota(jnp.int32, (1, 256), 1)

    def span(low):
        base = low // 128 * 128
        wide = 128 if low + head_dim <= base + 128 else 256
        mine = (lane[:, :wide] >= low - base) & (lane[:, :wide] < low - base + head_dim)
        return base, wide, mine

    def block(at, blocks, first):
        qr = pl.ds(pl.multiple_of(at * QUERY_ROWS, QUERY_ROWS), QUERY_ROWS)
        kr = pl.ds(pl.multiple_of(first * KEY_ROWS, KEY_ROWS), blocks * KEY_ROWS)
        query_mark = normed_ref[qr, width:]
        query_mark = jnp.concatenate([query_mark, query_mark], axis=1)
        key_mark = ((normed_ref[kr, width:].astype(F32) - 1.0) * -MASKED).astype(BF16)
        key_mark = jnp.concatenate([key_mark, key_mark], axis=1)
        for head in range(HEADS // 2):
            base, wide, mine = span(head * head_dim)
            queries = jnp.where(mine, qvk_s[qr, base : base + wide], query_mark[:, :wide])
            base += 2 * half
            keys = jnp.where(mine, qvk_s[kr, base : base + wide], key_mark[:, :wide])
            low = half + head * head_dim
            base, wide, mine = span(low)
            values = jnp.where(mine, qvk_s[kr, base : base + wide], jnp.ones((), BF16))
            scores = lax.dot_general(queries, keys, (((1,), (1,)), ((), ())), preferred_element_type=F32)
            top = jnp.max(scores, axis=1, keepdims=True)
            probs = jnp.exp2(scores - top).astype(BF16)
            out = jnp.dot(probs, values, preferred_element_type=F32)
            spare = 0 if low > base else wide - 1
            out = (out * (1.0 / out[:, spare : spare + 1])).astype(BF16)
            cols = slice(base - shift, base - shift + wide)
            old = jnp.zeros((), BF16) if head == 0 else context_ref[qr, cols]
            context_ref[qr, cols] = jnp.where(mine, out, old)

    def one_block(at, _):
        first = window_ref[0, at]
        blocks = window_ref[1, at]
        for size in (3, 4, 5, 6):

            @pl.when((blocks == size) if size > 3 else (blocks <= 3))
            def _():
                block(at, size, jnp.minimum(first, count // KEY_ROWS - size))

        return 0

    lax.fori_loop(0, count // QUERY_ROWS, one_block, 0)
    member = (segs_ref[...] == lax.broadcasted_iota(jnp.int32, (IMG_DEV, count), 0)).astype(F32)
    total = jnp.sum(member, axis=1, keepdims=True)
    sums = jnp.dot(member.astype(BF16), context_ref[:count, :], preferred_element_type=F32)
    context_ref[count:, :] = split(sums / total)


def key_windows(segs):
    blocks = segs.reshape(-1, QUERY_ROWS)
    start = jnp.sum((segs < blocks[:, :1]).astype(jnp.int32), axis=1)
    end = jnp.sum((segs <= blocks[:, -1:]).astype(jnp.int32), axis=1)
    first = start // KEY_ROWS
    return jnp.stack([first, (end + KEY_ROWS - 1) // KEY_ROWS - first])


def attend(place, segs, normed, shards):
    count = normed.shape[0]
    width = normed.shape[1] - 128
    columns = width // 2 * 3
    across = width // 2 + 64
    return pl.pallas_call(
        attend_kernel,
        grid=(1,),
        out_shape=jax.ShapeDtypeStruct((count + 2 * IMG_DEV, across), BF16),
        in_specs=[SMEM] * 2 + [whole(segs.shape)] + [ANY] * (len(shards) + 1),
        out_specs=whole((count + 2 * IMG_DEV, across)),
        scratch_shapes=[
            pltpu.VMEM(normed.shape, BF16),
            pltpu.VMEM((width, columns), BF16),
            pltpu.VMEM((count, columns + 64), BF16),
            pltpu.SemaphoreType.DMA((len(shards) + 1,)),
        ],
        compiler_params=params(),
        cost_estimate=cost(10**10, 2**24),
        name="attend",
    )(place, key_windows(segs), segs, normed, *shards)


def both_halves(place_ref, own, other):
    first = jnp.full(own.shape, place_ref[3], jnp.int32) == 0
    own, other = own.astype(F32), other.astype(F32)
    halves = [jnp.where(first, own, other), jnp.where(first, other, own)]
    return jnp.concatenate([part[:, 64:] for part in halves], axis=1).astype(BF16)


def pool_kernel(place_ref, rows_mean_ref, own_ref, other_ref, weight_ref, unit_ref, out_ref):
    context = both_halves(place_ref, own_ref[...], other_ref[...])
    pooled = rows_mean_ref[...] + join(jnp.dot(context, weight_ref[...], preferred_element_type=F32))
    unit = pooled * lax.rsqrt(jnp.sum(pooled * pooled, axis=1, keepdims=True) + 1e-06)
    unit_ref[...] = unit
    out_ref[...] = jnp.broadcast_to(unit.astype(BF16)[None], out_ref.shape)


def pool(place, rows_mean, own, other, rest, copies):
    images, width = rows_mean.shape
    last = own.shape[0] // (2 * images) - 1
    tail = pl.BlockSpec((2 * images, own.shape[1]), lambda i: (last, 0))
    return pl.pallas_call(
        pool_kernel,
        grid=(1,),
        out_shape=(jax.ShapeDtypeStruct((images, width), F32), jax.ShapeDtypeStruct((copies, images, width), BF16)),
        in_specs=[SMEM, whole((images, width)), tail, tail, whole((width, width))],
        out_specs=(whole((images, width)), whole((copies, images, width))),
        compiler_params=params(),
        cost_estimate=cost(2**25, 2**22),
        name="pool",
    )(place, rows_mean, own, other, rest)


def encode_kernel(place_ref, x_ref, own_ref, other_ref, weight_ref, out_ref):
    context = both_halves(place_ref, own_ref[...], other_ref[...])
    attended = jnp.dot(context, weight_ref[...], preferred_element_type=F32)
    out_ref[...] = (x_ref[...].astype(F32) + attended).astype(BF16)


def encode(place, x, own, other, rest):
    count, width = x.shape
    rows = 256
    block = pl.BlockSpec((rows, width), lambda i: (i, 0))
    half = pl.BlockSpec((rows, own.shape[1]), lambda i: (i, 0))
    return pl.pallas_call(
        encode_kernel,
        grid=(count // rows,),
        out_shape=jax.ShapeDtypeStruct((count, width), BF16),
        in_specs=[SMEM, block, half, half, pl.BlockSpec((width, width), lambda i: (0, 0))],
        out_specs=block,
        compiler_params=params(),
        cost_estimate=cost(3 * 10**9, 2**24),
        name="encode",
    )(place, x, own, other, rest)


def text_rows(packed, width):
    columns = width // 128
    texts = packed.shape[0] // columns
    packed = packed.astype(F32).reshape(texts // 8, columns * 8, 128)
    pieces = [packed[:, at * 8 : at * 8 + 8, :].reshape(texts, 128) for at in range(columns)]
    return jnp.concatenate(pieces, axis=1)


def inverse_norm(values):
    return lax.rsqrt(jnp.sum(values * values, axis=1, keepdims=True) + 1e-06)


def sigmoid_coeffs(logits, diagonal):
    sign = jnp.where(diagonal, 1.0, -1.0).astype(F32)
    return -10.0 * sign * jax.nn.sigmoid(-sign * logits)


def text_kernel(place_ref, units_ref, text_ref, out_ref):
    units = units_ref[...]
    images, width = units.shape
    text = text_rows(text_ref[...], width)
    texts = text.shape[0]
    scale = inverse_norm(text)
    dots = lax.dot_general(text.astype(BF16), units, (((1,), (1,)), ((), ())), preferred_element_type=F32)
    image = lax.broadcasted_iota(jnp.int32, (texts, images), 1) - place_ref[1] * IMG_DEV
    index = lax.broadcasted_iota(jnp.int32, (texts, images), 0) - place_ref[2] * IMG_DEV
    diagonal = (image == index) & (image >= 0) & (image < IMG_DEV)
    coeffs = sigmoid_coeffs(10.0 * dots * scale - 3.0, diagonal)
    out_ref[...] = join(jnp.dot(split(coeffs), units, preferred_element_type=F32)).astype(BF16)


def text_terms(place, units, rest):
    images, width = units.shape
    texts = rest.shape[0] * 128 // width
    return pl.pallas_call(
        text_kernel,
        grid=(1,),
        out_shape=jax.ShapeDtypeStruct((texts, width), BF16),
        in_specs=[SMEM, whole((images, width)), pl.BlockSpec((rest.shape[0], 128), lambda i: (0, width // 128))],
        out_specs=whole((texts, width)),
        compiler_params=params(),
        cost_estimate=cost(2**26, 2**21),
        name="text_terms",
    )(place, units, rest)


def image_kernel(place_ref, unit_ref, text_ref, out_ref):
    unit = unit_ref[...]
    images, width = unit.shape
    text = text_ref[...]
    texts = text.shape[0]
    scale = inverse_norm(text.astype(F32))
    dots = lax.dot_general(text, split(unit), (((1,), (1,)), ((), ())), preferred_element_type=F32)
    dots = dots[:, :images] + dots[:, images:]
    image = lax.broadcasted_iota(jnp.int32, (texts, images), 1) + place_ref[0] * images
    diagonal = image == lax.broadcasted_iota(jnp.int32, (texts, images), 0)
    coeffs = sigmoid_coeffs(10.0 * dots * scale - 3.0, diagonal) * scale
    out_ref[...] = join(jnp.dot(split(coeffs.T), text, preferred_element_type=F32))


def image_gradient(place, unit, text):
    return pl.pallas_call(
        image_kernel,
        grid=(1,),
        out_shape=jax.ShapeDtypeStruct(unit.shape, F32),
        in_specs=[SMEM, whole(unit.shape), whole(text.shape)],
        out_specs=whole(unit.shape),
        compiler_params=params(),
        cost_estimate=cost(2**28, 2**22),
        name="image_gradient",
    )(place, unit, text)


def gather_weights(own, beside):
    up, down, across, beside = lax.optimization_barrier(
        (take(own, FROM_UP), take(own, FROM_DOWN), take(own, FROM_ACROSS), beside)
    )
    far, across_up, across_down = lax.optimization_barrier(
        (take(up, FROM_UP), take(up, FROM_ACROSS), take(across, FROM_DOWN))
    )
    third = own.shape[0] // 3
    last = [
        take(far[:third], FROM_ACROSS),
        take(across_up[third : 2 * third], FROM_UP),
        take(across_down[2 * third :], FROM_DOWN),
    ]
    return [own, up, down, far, across, across_up, across_down] + last, beside


def body(
    patch_rows,
    segment_ids,
    norm_gain,
    query_weight,
    key_weight,
    value_weight,
    out_weight,
    text_embeds,
):
    count, width = patch_rows.shape
    n_row = lax.axis_size("row")
    n_col = lax.axis_size("col")
    row_at = lax.axis_index("row")
    col_at = lax.axis_index("col")
    core = col_at % 2
    y_at = col_at // 4
    z_hi = col_at // 2 % 2
    depth = query_weight.shape[0] * 2
    steps = [(0, 0), (1, 0), (-1, 0), (2, 0), (0, 1), (1, 1), (-1, 1), (2, 1)]
    firsts = [((y_at + dy) % SIDE * 2 + (z_hi + dz) % 2) * depth for dy, dz in steps]
    place = jnp.stack([col_at * n_row + row_at, row_at, col_at, core] + firsts).astype(jnp.int32)
    texts = text_embeds.shape[0]

    mine, other, rest, copies = pack(place, query_weight, key_weight, value_weight, out_weight, text_embeds, n_row)
    rest = lax.all_gather(rest, "col", axis=0, tiled=True)
    theirs = take(other, FROM_CORE)
    other_segs = take(segment_ids, FROM_CORE)
    own = jnp.where(core == 0, jnp.concatenate([mine, theirs]), jnp.concatenate([theirs, mine]))
    own, rows, other_segs, copies = lax.optimization_barrier((own, patch_rows, other_segs, copies))
    normed, rows_mean = norm(rows, norm_gain, segment_ids)
    column_text = lax.all_to_all(copies, "row", 0, 0)
    shards, (normed, column_text) = gather_weights(own, (normed, column_text))
    every_text = lax.all_gather(column_text.reshape(n_row * texts, width), "col", axis=0, tiled=True)
    other_normed = take(normed, FROM_CORE)
    for_other = attend(place, other_segs, other_normed, shards)
    context_other = take(for_other, FROM_CORE)
    context_own = attend(place, segment_ids, normed, shards)
    context_own, rest = lax.optimization_barrier((context_own, rest))
    unit, units = pool(place, rows_mean, context_own, context_other, rest, n_row)
    units = lax.all_to_all(units, "row", 0, 0)
    encoded = encode(place, patch_rows, context_own, context_other, rest)
    units, encoded = lax.optimization_barrier((units, encoded))
    terms = text_terms(place, units.reshape(n_row * IMG_DEV, width), rest)
    terms, unit, every_text = lax.optimization_barrier((terms, unit, every_text))
    terms = lax.all_to_all(terms.reshape(n_col, texts, width), "col", 0, 0)
    image_grad = image_gradient(place, unit, every_text)
    return (encoded, image_grad, jnp.sum(terms.astype(F32), axis=0))


def solution(mesh):
    return jax.shard_map(
        body,
        mesh=mesh,
        in_specs=(
            P(("row", "col"), None),
            P(("row", "col"), None),
            P(),
            P("col", None),
            P("col", None),
            P("col", None),
            P("col", None),
            P(("row", "col"), None),
        ),
        out_specs=(P(("row", "col"), None), P(("row", "col"), None), P(("row", "col"), None)),
        check_vma=False,
    )
```

time: 595 us -> 156 us (0.26)
  waiting for transfers between devices: 448 us -> 29.5 us
  matrix products: 108 us -> 0 us
  Pallas kernels: 0 us -> 63.5 us
  starting transfers between devices: 0.23 us -> 38.4 us
  local copies, waits for them, and re-layouts: 16.5 us -> 4.67 us
    all_gather x5 -> x2, waiting for transfers between devices: 296 us -> 0.02 us  [the longest x1 0.02 us: body(): rest = lax.all_gather(rest, 'col', axis=0, tiled=True)]
    unnamed x7 -> x2, waiting for transfers between devices: 152 us -> 0.03 us
    dot_general x10 -> x0, matrix products: 72.3 us -> none  [the longest x2 29.5 us: body(): jnp.einsum('hqk,khd->qhd', probs, vh, preferred_element_type=jnp.float32)]
    pallas_call x0 -> x8, Pallas kernels: none -> 63.5 us  [the longest x2 38.3 us: attend(): pl.pallas_call(attend_kernel, grid=(1,), out_shape=jax.ShapeDtypeStruct((...]
    sub x2 -> x0, matrix products: 35.7 us -> none  [body(): expo = jnp.exp(scores - top)]
    ppermute x0 -> x13, waiting for transfers between devices: none -> 24.4 us  [take(): return lax.ppermute(values, AXES, found)]
    ppermute x0 -> x13, starting transfers between devices: none -> 24.1 us  [take(): return lax.ppermute(values, AXES, found)]
    all_to_all x0 -> x3, starting transfers between devices: none -> 14.3 us  [the longest x1 6.17 us: body(): terms = lax.all_to_all(terms.reshape(n_col, texts, width), 'col', 0, 0)]
  transfers between devices with their start and end apart: 6 -> 18, of which waited for: 6 -> 7; matrix products, arithmetic and copies ran while one was open for 20% -> 4% of each run, Pallas kernels for 0% -> 39%
where the time goes in v2:
time: 156 us; the launch traced here: 155 us
  Pallas kernels  63.5 us (41%)
  starting transfers between devices  38.4 us (25%)
  waiting for transfers between devices  29.5 us (19%)
  between operations  14.4 us (9%)
  other arithmetic  4.77 us (3%)
  local copies, waits for them, and re-layouts  4.67 us (3%)
    pallas_call x2, Pallas kernels, attend(): pl.pallas_call(attend_kernel, grid=(1,), out_shape=jax.ShapeDtypeStruct((...  38.3 us
    ppermute x13, waiting for transfers between devices, take(): return lax.ppermute(values, AXES, found)  24.4 us
    ppermute x13, starting transfers between devices, take(): return lax.ppermute(values, AXES, found)  24.1 us
    pallas_call x1, Pallas kernels, encode(): pl.pallas_call(encode_kernel, grid=(count // rows,), out_shape=jax.ShapeD...  7.71 us
    all_to_all x1, starting transfers between devices, body(): terms = lax.all_to_all(terms.reshape(n_col, texts, width), 'col', 0, 0)  6.17 us
    pallas_call x1, Pallas kernels, norm(): pl.pallas_call(norm_kernel, grid=(1,), out_shape=(jax.ShapeDtypeStruct((c...  5.5 us
    all_to_all x1, waiting for transfers between devices, body(): terms = lax.all_to_all(terms.reshape(n_col, texts, width), 'col', 0, 0)  4.96 us
    pallas_call x1, Pallas kernels, image_gradient(): pl.pallas_call(image_kernel, grid=(1,), out_shape=jax.ShapeDtypeStruct(un...  4.26 us
  transfers between devices with their start and end apart: 18, of which 7 were waited for; matrix products, arithmetic and copies ran while one was open for 4% of the time, Pallas kernels for 39%

profile of v2, /device:TPU:1, one launch (start us, length us, event | category | flops | bytes accessed | tf_op | source)
XLA Modules:
  0.0 155.2 jit_solution(3620692458491829543)
XLA Ops:
  8.0 2.2 %pack.1 = (bf16[72,1728]{1,0:T(8,128)(2,1)}, bf16[72,1728]{1,0:T(8,128)(2,1)}, bf16[72,1280]{1,0:T(8,128)(2,1)}, bf16[8,8,1152]{2,1,0:T(8,128)(2,1)}) custom-call(s32[12]{0:T(128)} %stack.61.place_ref, bf16[72,1152]{1,0:T(8,128)(2,1)} %q_ref.1, bf16[72,1152]{1,0:T(8,128)(2,1)} %k_ref.1, bf16[72,1152]{1,0:T(8,128)(2,1)} %v_ref.1, bf16[72,1152]{1,0:T(8,128)(2,1)} %o_ref.1, ...), custom_call_target="tpu_custom_call" | custom-call | bytes 2097152 | tf_op jit(solution)/shard_map/pack/pallas_call | solution.py:83
  10.2 1.5 collective-permute-start
  14.3 2.9 %collective-permute-start.2 = (bf16[144,1728]{1,0:T(8,128)(2,1)S(1)}, bf16[144,1728]{1,0:T(8,128)(2,1)S(1)}, u32[]{:S(2)}, u32[]{:S(2)}) collective-permute-start(bf16[144,1728]{1,0:T(8,128)(2,1)S(1)} %maximum_select_fusion.refs_0_), channel_id=1, source_target_pairs={{4,0},{5,1},{20,16},{21,17},{6,2},{7,3},{22,18},{23,19},{8,4},{9,5... | collective-permute-start | bytes 1493000 | tf_op jit(solution)/shard_map/ppermute | solution.py:57
  17.2 3.8 %collective-permute-start.4 = (bf16[144,1728]{1,0:T(8,128)(2,1)S(1)}, bf16[144,1728]{1,0:T(8,128)(2,1)S(1)}, u32[]{:S(2)}, u32[]{:S(2)}) collective-permute-start(bf16[144,1728]{1,0:T(8,128)(2,1)S(1)} %maximum_select_fusion.refs_0_), channel_id=1, source_target_pairs={{18,0},{19,1},{2,16},{3,17},{16,2},{17,3},{0,18},{1,19},{22,4},{23... | collective-permute-start | bytes 1493000 | tf_op jit(solution)/shard_map/ppermute | solution.py:57
  21.0 4.0 %all-to-all-start = ((bf16[8,8,1152]{2,1,0:T(8,128)(2,1)}), bf16[8,8,1152]{2,1,0:T(8,128)(2,1)S(1)}, u32[]{:S(2)}, u32[]{:S(2)}) async-start(bf16[8,8,1152]{2,1,0:T(8,128)(2,1)} %get-tuple-element.37), calls=%async_computation | async-start | bytes 294912 | tf_op jit(solution)/shard_map/all_to_all | solution.py:429
  25.6 5.5 %norm.1 = (bf16[1024,1280]{1,0:T(8,128)(2,1)}, f32[8,1152]{1,0:T(8,128)}) custom-call(bf16[1024,1152]{1,0:T(8,128)(2,1)} %x_ref.2, f32[1,1152]{1,0:T(1,128)} %reshape.244.gain_ref, s32[1,1024]{1,0:T(1,128)} %segs_ref.3), custom_call_target="tpu_custom_call" | custom-call | bytes 16777216 | tf_op jit(solution)/shard_map/norm/pallas_call | solution.py:117
  32.3 2.1 %collective-permute-done.4.refs_4_ = bf16[144,1728]{1,0:T(8,128)(2,1)S(1)} collective-permute-done((bf16[144,1728]{1,0:T(8,128)(2,1)S(1)}, bf16[144,1728]{1,0:T(8,128)(2,1)S(1)}, u32[]{:S(2)}, u32[]{:S(2)}) %collective-permute-start.4) | collective-permute-done | bytes 497696 | tf_op jit(solution)/shard_map/ppermute | solution.py:57
  36.9 2.7 %collective-permute-start.5 = (bf16[144,1728]{1,0:T(8,128)(2,1)S(1)}, bf16[144,1728]{1,0:T(8,128)(2,1)S(1)}, u32[]{:S(2)}, u32[]{:S(2)}) collective-permute-start(bf16[144,1728]{1,0:T(8,128)(2,1)S(1)} %collective-permute-done.2.refs_1_), channel_id=1, source_target_pairs={{4,0},{5,1},{20,16},{21,17},{6,2},{7,3},{22,18},{23,19},{8,4},{9,5... | collective-permute-start | bytes 1493000 | tf_op jit(solution)/shard_map/ppermute | solution.py:57
  39.6 2.7 %collective-permute-start.6 = (bf16[144,1728]{1,0:T(8,128)(2,1)S(1)}, bf16[144,1728]{1,0:T(8,128)(2,1)S(1)}, u32[]{:S(2)}, u32[]{:S(2)}) collective-permute-start(bf16[144,1728]{1,0:T(8,128)(2,1)S(1)} %collective-permute-done.2.refs_1_), channel_id=1, source_target_pairs={{18,0},{19,1},{2,16},{3,17},{16,2},{17,3},{0,18},{1,19},{22,4},{23... | collective-permute-start | bytes 1493000 | tf_op jit(solution)/shard_map/ppermute | solution.py:57
  43.7 9.3 %collective-permute-done.5.refs_3_ = bf16[144,1728]{1,0:T(8,128)(2,1)S(1)} collective-permute-done((bf16[144,1728]{1,0:T(8,128)(2,1)S(1)}, bf16[144,1728]{1,0:T(8,128)(2,1)S(1)}, u32[]{:S(2)}, u32[]{:S(2)}) %collective-permute-start.5) | collective-permute-done | bytes 497696 | tf_op jit(solution)/shard_map/ppermute | solution.py:57
  53.0 8.9 %collective-permute-done.6.refs_5_ = bf16[144,1728]{1,0:T(8,128)(2,1)S(1)} collective-permute-done((bf16[144,1728]{1,0:T(8,128)(2,1)S(1)}, bf16[144,1728]{1,0:T(8,128)(2,1)S(1)}, u32[]{:S(2)}, u32[]{:S(2)}) %collective-permute-start.6) | collective-permute-done | bytes 497696 | tf_op jit(solution)/shard_map/ppermute | solution.py:57
  62.0 2.6 %collective-permute-start.8 = (bf16[48,1728]{1,0:T(8,128)(2,1)S(1)}, bf16[48,1728]{1,0:T(8,128)(2,1)S(1)}, u32[]{:S(2)}, u32[]{:S(2)}) collective-permute-start(bf16[48,1728]{1,0:T(8,128)(2,1)S(1)} %slice.23), channel_id=1, source_target_pairs={{18,0},{19,1},{2,16},{3,17},{16,2},{17,3},{0,18},{1,19},{22,4},{23... | collective-permute-start | bytes 497672 | tf_op jit(solution)/shard_map/ppermute | solution.py:57
  64.6 2.9 %collective-permute-start.9 = (bf16[48,1728]{1,0:T(8,128)(2,1)S(1)}, bf16[48,1728]{1,0:T(8,128)(2,1)S(1)}, u32[]{:S(2)}, u32[]{:S(2)}) collective-permute-start(bf16[48,1728]{1,0:T(8,128)(2,1)S(1)} %slice.24), channel_id=1, source_target_pairs={{4,0},{5,1},{20,16},{21,17},{6,2},{7,3},{22,18},{23,19},{8,4},{9,5... | collective-permute-start | bytes 497672 | tf_op jit(solution)/shard_map/ppermute | solution.py:57
  68.1 1.7 %collective-permute-done.9.refs_8_ = bf16[48,1728]{1,0:T(8,128)(2,1)S(1)} collective-permute-done((bf16[48,1728]{1,0:T(8,128)(2,1)S(1)}, bf16[48,1728]{1,0:T(8,128)(2,1)S(1)}, u32[]{:S(2)}, u32[]{:S(2)}) %collective-permute-start.9) | collective-permute-done | bytes 165920 | tf_op jit(solution)/shard_map/ppermute | solution.py:57
  70.5 18.8 %attend.3 = bf16[1040,640]{1,0:T(8,128)(2,1)} custom-call(s32[12]{0:T(128)} %stack.61.place_ref, s32[2,4]{1,0:T(2,128)} %pad_add_fusion.1.window_ref, s32[1,1024]{1,0:T(1,128)} %copy-done.8, bf16[1024,1280]{1,0:T(8,128)(2,1)} %collective-permute-done.11.normed_hbm, bf16[144,1728]{1,0:T(8,128)(2,1)} %copy-done.3, bf16[144,1728]{1,0:T(8,128)(2,1)} %copy-done.10, ...), custom_call_target="tpu_custom_call" | custom-call | flops 10000000000 | bytes 16777216 | tf_op jit(solution)/shard_map/attend/pallas_call | solution.py:237
  89.4 3.6 %collective-permute-start.12 = (bf16[1040,640]{1,0:T(8,128)(2,1)}, bf16[1040,640]{1,0:T(8,128)(2,1)S(1)}, u32[]{:S(2)}, u32[]{:S(2)}) collective-permute-start(bf16[1040,640]{1,0:T(8,128)(2,1)} %attend.3), channel_id=1, source_target_pairs={{1,0},{0,1},{17,16},{16,17},{3,2},{2,3},{19,18},{18,19},{5,4},{4,5... | collective-permute-start | bytes 3993608 | tf_op jit(solution)/shard_map/ppermute | solution.py:57
  93.7 19.5 %attend.2.own_ref = bf16[1040,640]{1,0:T(8,128)(2,1)} custom-call(s32[12]{0:T(128)} %stack.61.place_ref, s32[2,4]{1,0:T(2,128)} %pad_add_fusion.window_ref, s32[1,1024]{1,0:T(1,128)} %segs_ref.3, bf16[1024,1280]{1,0:T(8,128)(2,1)} %get-tuple-element.38.normed_hbm, bf16[144,1728]{1,0:T(8,128)(2,1)} %copy-done.3, bf16[144,1728]{1,0:T(8,128)(2,1)} %copy-done.10, ...), custom_call_target="tpu_custom_call" | custom-call | flops 10000000000 | bytes 16777216 | tf_op jit(solution)/shard_map/attend/pallas_call | solution.py:237
  114.4 3.1 %pool.1 = (f32[8,1152]{1,0:T(8,128)}, bf16[8,8,1152]{2,1,0:T(8,128)(2,1)}) custom-call(s32[12]{0:T(128)} %stack.61.place_ref, f32[8,1152]{1,0:T(8,128)} %get-tuple-element.34.rows_mean_ref, bf16[1040,640]{1,0:T(8,128)(2,1)} %attend.2.own_ref, bf16[1040,640]{1,0:T(8,128)(2,1)} %copy-done, bf16[1152,1280]{1,0:T(8,128)(2,1)} %all-gather.3.cloned.1.call-done.weight_ref.text_ref), custom_call_target="tpu_custom_call" | custom-call | flops 33554432 | bytes 4194304 | tf_op jit(solution)/shard_map/pool/pallas_call | solution.py:274
  117.5 4.1 %all-to-all-start.1 = ((bf16[8,8,1152]{2,1,0:T(8,128)(2,1)}), bf16[8,8,1152]{2,1,0:T(8,128)(2,1)S(1)}, u32[]{:S(2)}, u32[]{:S(2)}) async-start(bf16[8,8,1152]{2,1,0:T(8,128)(2,1)} %get-tuple-element.49), calls=%async_computation.1 | async-start | bytes 294912 | tf_op jit(solution)/shard_map/all_to_all | solution.py:438
  121.6 7.7 %encode.1 = bf16[1024,1152]{1,0:T(8,128)(2,1)} custom-call(s32[12]{0:T(128)} %stack.61.place_ref, bf16[1024,1152]{1,0:T(8,128)(2,1)} %x_ref.2, bf16[1040,640]{1,0:T(8,128)(2,1)} %attend.2.own_ref, bf16[1040,640]{1,0:T(8,128)(2,1)} %copy-done, bf16[1152,1280]{1,0:T(8,128)(2,1)} %all-gather.3.cloned.1.call-done.weight_ref.text_ref), custom_call_target="tpu_custom_call" | custom-call | flops 3000000000 | bytes 16777216 | tf_op jit(solution)/shard_map/encode/pallas_call | solution.py:297
  130.0 2.4 %text_terms.1 = bf16[128,1152]{1,0:T(8,128)(2,1)} custom-call(s32[12]{0:T(128)} %stack.61.place_ref, bf16[64,1152]{1,0:T(8,128)(2,1)} %bitcast.62, bf16[1152,1280]{1,0:T(8,128)(2,1)} %all-gather.3.cloned.1.call-done.weight_ref.text_ref), custom_call_target="tpu_custom_call" | custom-call | flops 67108864 | bytes 2097152 | tf_op jit(solution)/shard_map/text_terms/pallas_call | solution.py:343
  132.4 6.2 %all-to-all-start.2 = ((bf16[16,8,1152]{2,1,0:T(8,128)(2,1)}), bf16[16,8,1152]{2,1,0:T(8,128)(2,1)S(1)}, u32[]{:S(2)}, u32[]{:S(2)}) async-start(bf16[16,8,1152]{2,1,0:T(8,128)(2,1)} %bitcast.61), calls=%async_computation.2 | async-start | bytes 589824 | tf_op jit(solution)/shard_map/all_to_all | solution.py:443
  138.5 4.3 %image_gradient.1 = f32[8,1152]{1,0:T(8,128)} custom-call(s32[12]{0:T(128)} %stack.61.place_ref, f32[8,1152]{1,0:T(8,128)} %get-tuple-element.54.unit_ref, bf16[1024,1152]{1,0:T(8,128)(2,1)} %all-gather.5.cloned.1.call-done.text_ref), custom_call_target="tpu_custom_call" | custom-call | flops 268435456 | bytes 4194304 | tf_op jit(solution)/shard_map/image_gradient/pallas_call | solution.py:370
  142.8 5.0 %all-to-all-done.2 = bf16[16,8,1152]{2,1,0:T(8,128)(2,1)S(1)} async-done(((bf16[16,8,1152]{2,1,0:T(8,128)(2,1)}), bf16[16,8,1152]{2,1,0:T(8,128)(2,1)S(1)}, u32[]{:S(2)}, u32[]{:S(2)}) %all-to-all-start.2) | async-done | bytes 294944 | tf_op jit(solution)/shard_map/all_to_all | solution.py:443
  (78 shorter events, 13.4 us)
Async XLA Ops:
  7.2 17.9 %copy-start.9 = (f32[1152]{0:T(1024)S(1)}, f32[1152]{0:T(1024)}, u32[]{:S(2)}) copy-start(f32[1152]{0:T(1024)} %param.10) | copy-start | bytes 13828
  7.2 106.1 %all-gather.3.cloned.1.call-start = ((), (), s32[]{:S(2)}) async-start(), calls=%async_computation.3 | async-start | bytes 3133440 | tf_op jit(solution)/shard_map/all_gather | solution.py:423
  8.0 28.2 %copy-start.7 = (s32[1,1024]{1,0:T(1,128)S(1)}, s32[1,1024]{1,0:T(1,128)}, u32[]{:S(2)}) copy-start(s32[1,1024]{1,0:T(1,128)} %segs_ref.3) | copy-start | bytes 12292
  10.2 2.9 %collective-permute-start = (bf16[72,1728]{1,0:T(8,128)(2,1)}, bf16[72,1728]{1,0:T(8,128)(2,1)S(1)}, u32[]{:S(2)}, u32[]{:S(2)}) collective-permute-start(bf16[72,1728]{1,0:T(8,128)(2,1)} %get-tuple-element.31), channel_id=1, source_target_pairs={{1,0},{0,1},{17,16},{16,17},{3,2},{2,3},{19,18},{18,19},{5,4},{4,5... | collective-permute-start | bytes 746504 | tf_op jit(solution)/shard_map/ppermute | solution.py:57
  11.7 2.6 %collective-permute-start.1 = (s32[1,1024]{1,0:T(1,128)}, s32[1,1024]{1,0:T(1,128)S(1)}, u32[]{:S(2)}, u32[]{:S(2)}) collective-permute-start(s32[1,1024]{1,0:T(1,128)} %segs_ref.3), channel_id=1, source_target_pairs={{1,0},{0,1},{17,16},{16,17},{3,2},{2,3},{19,18},{18,19},{5,4},{4,5... | collective-permute-start | bytes 12296 | tf_op jit(solution)/shard_map/ppermute | solution.py:57
  14.3 55.6 %copy-start.3 = (bf16[144,1728]{1,0:T(8,128)(2,1)}, bf16[144,1728]{1,0:T(8,128)(2,1)S(1)}, u32[]{:S(2)}) copy-start(bf16[144,1728]{1,0:T(8,128)(2,1)S(1)} %maximum_select_fusion.refs_0_) | copy-start | bytes 1492996
  14.3 55.6 %copy-start.8 = (s32[1,1024]{1,0:T(1,128)}, s32[1,1024]{1,0:T(1,128)S(1)}, u32[]{:S(2)}) copy-start(s32[1,1024]{1,0:T(1,128)S(1)} %collective-permute-done.1.segs_ref) | copy-start | bytes 12292
  14.3 16.8 %collective-permute-start.2 = (bf16[144,1728]{1,0:T(8,128)(2,1)S(1)}, bf16[144,1728]{1,0:T(8,128)(2,1)S(1)}, u32[]{:S(2)}, u32[]{:S(2)}) collective-permute-start(bf16[144,1728]{1,0:T(8,128)(2,1)S(1)} %maximum_select_fusion.refs_0_), channel_id=1, source_target_pairs={{4,0},{5,1},{20,16},{21,17},{6,2},{7,3},{22,18},{23,19},{8,4},{9,5... | collective-permute-start | bytes 1493000 | tf_op jit(solution)/shard_map/ppermute | solution.py:57
  17.2 15.1 %collective-permute-start.3 = (bf16[144,1728]{1,0:T(8,128)(2,1)S(1)}, bf16[144,1728]{1,0:T(8,128)(2,1)S(1)}, u32[]{:S(2)}, u32[]{:S(2)}) collective-permute-start(bf16[144,1728]{1,0:T(8,128)(2,1)S(1)} %maximum_select_fusion.refs_0_), channel_id=1, source_target_pairs={{12,0},{13,1},{28,16},{29,17},{14,2},{15,3},{30,18},{31,19},{0,4},... | collective-permute-start | bytes 1493000 | tf_op jit(solution)/shard_map/ppermute | solution.py:57
  17.2 17.2 %collective-permute-start.4 = (bf16[144,1728]{1,0:T(8,128)(2,1)S(1)}, bf16[144,1728]{1,0:T(8,128)(2,1)S(1)}, u32[]{:S(2)}, u32[]{:S(2)}) collective-permute-start(bf16[144,1728]{1,0:T(8,128)(2,1)S(1)} %maximum_select_fusion.refs_0_), channel_id=1, source_target_pairs={{18,0},{19,1},{2,16},{3,17},{16,2},{17,3},{0,18},{1,19},{22,4},{23... | collective-permute-start | bytes 1493000 | tf_op jit(solution)/shard_map/ppermute | solution.py:57
  21.0 10.2 %all-to-all-start = ((bf16[8,8,1152]{2,1,0:T(8,128)(2,1)}), bf16[8,8,1152]{2,1,0:T(8,128)(2,1)S(1)}, u32[]{:S(2)}, u32[]{:S(2)}) async-start(bf16[8,8,1152]{2,1,0:T(8,128)(2,1)} %get-tuple-element.37), calls=%async_computation | async-start | bytes 294912 | tf_op jit(solution)/shard_map/all_to_all | solution.py:429
  25.0 107.4 %all-gather.5.cloned.1.call-start = ((), (), s32[]{:S(2)}) async-start(), calls=%async_computation.4 | async-start | bytes 2506752 | tf_op jit(solution)/shard_map/all_gather | solution.py:431
  31.1 38.8 %copy-start.10 = (bf16[144,1728]{1,0:T(8,128)(2,1)}, bf16[144,1728]{1,0:T(8,128)(2,1)S(1)}, u32[]{:S(2)}) copy-start(bf16[144,1728]{1,0:T(8,128)(2,1)S(1)} %collective-permute-done.2.refs_1_) | copy-start | bytes 1492996
  32.3 37.6 %copy-start.11 = (bf16[144,1728]{1,0:T(8,128)(2,1)}, bf16[144,1728]{1,0:T(8,128)(2,1)S(1)}, u32[]{:S(2)}) copy-start(bf16[144,1728]{1,0:T(8,128)(2,1)S(1)} %collective-permute-done.3.refs_2_) | copy-start | bytes 1492996
  34.4 35.4 %collective-permute-start.11 = (bf16[1024,1280]{1,0:T(8,128)(2,1)}, bf16[1024,1280]{1,0:T(8,128)(2,1)}, u32[]{:S(2)}, u32[]{:S(2)}) collective-permute-start(bf16[1024,1280]{1,0:T(8,128)(2,1)} %get-tuple-element.38.normed_hbm), channel_id=1, source_target_pairs={{1,0},{0,1},{17,16},{16,17},{3,2},{2,3},{19,18},{18,19},{5,4},{4,5... | collective-permute-start | bytes 7864328 | tf_op jit(solution)/shard_map/ppermute | solution.py:57
  36.9 16.1 %collective-permute-start.5 = (bf16[144,1728]{1,0:T(8,128)(2,1)S(1)}, bf16[144,1728]{1,0:T(8,128)(2,1)S(1)}, u32[]{:S(2)}, u32[]{:S(2)}) collective-permute-start(bf16[144,1728]{1,0:T(8,128)(2,1)S(1)} %collective-permute-done.2.refs_1_), channel_id=1, source_target_pairs={{4,0},{5,1},{20,16},{21,17},{6,2},{7,3},{22,18},{23,19},{8,4},{9,5... | collective-permute-start | bytes 1493000 | tf_op jit(solution)/shard_map/ppermute | solution.py:57
  39.6 22.2 %collective-permute-start.6 = (bf16[144,1728]{1,0:T(8,128)(2,1)S(1)}, bf16[144,1728]{1,0:T(8,128)(2,1)S(1)}, u32[]{:S(2)}, u32[]{:S(2)}) collective-permute-start(bf16[144,1728]{1,0:T(8,128)(2,1)S(1)} %collective-permute-done.2.refs_1_), channel_id=1, source_target_pairs={{18,0},{19,1},{2,16},{3,17},{16,2},{17,3},{0,18},{1,19},{22,4},{23... | collective-permute-start | bytes 1493000 | tf_op jit(solution)/shard_map/ppermute | solution.py:57
  42.3 19.5 %collective-permute-start.7 = (bf16[144,1728]{1,0:T(8,128)(2,1)}, bf16[144,1728]{1,0:T(8,128)(2,1)S(1)}, u32[]{:S(2)}, u32[]{:S(2)}) collective-permute-start(bf16[144,1728]{1,0:T(8,128)(2,1)} %copy-done.12), channel_id=1, source_target_pairs={{12,0},{13,1},{28,16},{29,17},{14,2},{15,3},{30,18},{31,19},{0,4},... | collective-permute-start | bytes 1493000 | tf_op jit(solution)/shard_map/ppermute | solution.py:57
  61.8 6.3 %collective-permute-start.10 = (bf16[48,1728]{1,0:T(8,128)(2,1)S(1)}, bf16[48,1728]{1,0:T(8,128)(2,1)S(1)}, u32[]{:S(2)}, u32[]{:S(2)}) collective-permute-start(bf16[48,1728]{1,0:T(8,128)(2,1)S(1)} %slice.25), channel_id=1, source_target_pairs={{12,0},{13,1},{28,16},{29,17},{14,2},{15,3},{30,18},{31,19},{0,4},... | collective-permute-start | bytes 497672 | tf_op jit(solution)/shard_map/ppermute | solution.py:57
  62.0 6.2 %collective-permute-start.8 = (bf16[48,1728]{1,0:T(8,128)(2,1)S(1)}, bf16[48,1728]{1,0:T(8,128)(2,1)S(1)}, u32[]{:S(2)}, u32[]{:S(2)}) collective-permute-start(bf16[48,1728]{1,0:T(8,128)(2,1)S(1)} %slice.23), channel_id=1, source_target_pairs={{18,0},{19,1},{2,16},{3,17},{16,2},{17,3},{0,18},{1,19},{22,4},{23... | collective-permute-start | bytes 497672 | tf_op jit(solution)/shard_map/ppermute | solution.py:57
  64.6 5.3 %collective-permute-start.9 = (bf16[48,1728]{1,0:T(8,128)(2,1)S(1)}, bf16[48,1728]{1,0:T(8,128)(2,1)S(1)}, u32[]{:S(2)}, u32[]{:S(2)}) collective-permute-start(bf16[48,1728]{1,0:T(8,128)(2,1)S(1)} %slice.24), channel_id=1, source_target_pairs={{4,0},{5,1},{20,16},{21,17},{6,2},{7,3},{22,18},{23,19},{8,4},{9,5... | collective-permute-start | bytes 497672 | tf_op jit(solution)/shard_map/ppermute | solution.py:57
  89.4 24.0 %collective-permute-start.12 = (bf16[1040,640]{1,0:T(8,128)(2,1)}, bf16[1040,640]{1,0:T(8,128)(2,1)S(1)}, u32[]{:S(2)}, u32[]{:S(2)}) collective-permute-start(bf16[1040,640]{1,0:T(8,128)(2,1)} %attend.3), channel_id=1, source_target_pairs={{1,0},{0,1},{17,16},{16,17},{3,2},{2,3},{19,18},{18,19},{5,4},{4,5... | collective-permute-start | bytes 3993608 | tf_op jit(solution)/shard_map/ppermute | solution.py:57
  117.5 11.8 %all-to-all-start.1 = ((bf16[8,8,1152]{2,1,0:T(8,128)(2,1)}), bf16[8,8,1152]{2,1,0:T(8,128)(2,1)S(1)}, u32[]{:S(2)}, u32[]{:S(2)}) async-start(bf16[8,8,1152]{2,1,0:T(8,128)(2,1)} %get-tuple-element.49), calls=%async_computation.1 | async-start | bytes 294912 | tf_op jit(solution)/shard_map/all_to_all | solution.py:438
  132.4 15.4 %all-to-all-start.2 = ((bf16[16,8,1152]{2,1,0:T(8,128)(2,1)}), bf16[16,8,1152]{2,1,0:T(8,128)(2,1)S(1)}, u32[]{:S(2)}, u32[]{:S(2)}) async-start(bf16[16,8,1152]{2,1,0:T(8,128)(2,1)} %bitcast.61), calls=%async_computation.2 | async-start | bytes 589824 | tf_op jit(solution)/shard_map/all_to_all | solution.py:443
  (10 other events, 46.2 us)
Sparse Core Ops, SparseCore 0:
  10.3 56.2 all-gather.2
  69.0 48.0 all-gather.4

commit v3 on v2

--- a/solution.py
+++ b/solution.py
@@ -12,6 +12,7 @@
 MASKED = -1e30
 QUERY_ROWS = 256
 KEY_ROWS = 128
+PROJECT_CHUNKS = 4
 SIDE = 4
 AXES = ("row", "col")
 F32 = jnp.float32
@@ -47,6 +48,7 @@
     return found
 
 
+SAME_CORE = [list(range(core, 16, 2)) for core in range(2)]
 FROM_CORE = pairs(lambda x, y, z, core: (x, y, z, 1 - core))
 FROM_UP = pairs(lambda x, y, z, core: (x, y + 1, z, core))
 FROM_DOWN = pairs(lambda x, y, z, core: (x, y - 1, z, core))
@@ -57,39 +59,51 @@
     return lax.ppermute(values, AXES, found)
 
 
-def pack_kernel(place_ref, q_ref, k_ref, v_ref, o_ref, text_ref, mine_ref, other_ref, rest_ref, copies_ref):
+def pack_kernel(place_ref, q_ref, k_ref, v_ref, mine_ref, other_ref):
     width = q_ref.shape[1]
-    half = width // 2
-
-    def columns(at):
-        cols = slice(at * half, (at + 1) * half)
-        return jnp.concatenate([q_ref[:, cols], v_ref[:, cols], k_ref[:, cols]], axis=1)
+    head_dim = width // HEADS
+
+    def columns(core):
+        cols = [slice(head * head_dim, (head + 1) * head_dim) for head in range(core, HEADS, 2)]
+        return jnp.concatenate([ref[:, col] for ref in (q_ref, v_ref, k_ref) for col in cols], axis=1)
 
     first, second = columns(0), columns(1)
     core = jnp.full(first.shape, place_ref[3], jnp.int32) == 0
     mine_ref[...] = jnp.where(core, first.astype(F32), second.astype(F32)).astype(BF16)
     other_ref[...] = jnp.where(core, second.astype(F32), first.astype(F32)).astype(BF16)
-    rest_ref[:, :width] = o_ref[...]
-    text = text_ref[...].astype(F32)
-    blocks = [text[:, at : at + 128] for at in range(0, width, 128)]
-    rest_ref[:, width:] = jnp.concatenate(blocks, axis=0).astype(BF16)
-    copies_ref[...] = jnp.broadcast_to(text_ref[...][None], copies_ref.shape)
-
-
-def pack(place, q, k, v, o, text, copies):
+
+
+def pack(place, q, k, v):
     depth, width = q.shape
     part = (depth, width // 2 * 3)
-    outs = (part, part, (depth, width + 128), (copies,) + text.shape)
     return pl.pallas_call(
         pack_kernel,
         grid=(1,),
-        out_shape=tuple(jax.ShapeDtypeStruct(out, BF16) for out in outs),
-        in_specs=[SMEM] + [whole(values.shape) for values in (q, k, v, o, text)],
-        out_specs=tuple(whole(out) for out in outs),
+        out_shape=(jax.ShapeDtypeStruct(part, BF16),) * 2,
+        in_specs=[SMEM] + [whole(q.shape)] * 3,
+        out_specs=(whole(part),) * 2,
         compiler_params=params(),
         cost_estimate=cost(0, 2**21),
         name="pack",
-    )(place, q, k, v, o, text)
+    )(place, q, k, v)
+
+
+def copies_kernel(in_ref, out_ref):
+    out_ref[...] = jnp.broadcast_to(in_ref[...][None], out_ref.shape)
+
+
+def copies_of(values, copies):
+    out = (copies,) + values.shape
+    return pl.pallas_call(
+        copies_kernel,
+        grid=(1,),
+        out_shape=jax.ShapeDtypeStruct(out, BF16),
+        in_specs=[whole(values.shape)],
+        out_specs=whole(out),
+        compiler_params=params(),
+        cost_estimate=cost(0, 2**22),
+        name="copies",
+    )(values)
 
 
 def norm_kernel(x_ref, gain_ref, segs_ref, out_ref, mean_ref):
@@ -147,7 +161,9 @@
     head_dim = width // HEADS
     shift = half // 128 * 128
 
-    copies = [pltpu.make_async_copy(normed_hbm, normed_ref, sems.at[len(shards)])]
+    chunk = count // PROJECT_CHUNKS
+
+    copies = []
     for at, shard in enumerate(shards):
         whole = min(at, 7)
         row = place_ref[4 + whole]
@@ -157,6 +173,13 @@
         copies.append(pltpu.make_async_copy(shard, weight_s.at[rows, :], sems.at[at]))
     for copy in copies:
         copy.start()
+
+    def normed_copy(i):
+        rows = pl.ds(pl.multiple_of(i * chunk, chunk), chunk)
+        return pltpu.make_async_copy(normed_hbm.at[rows, :], normed_ref.at[rows, :], sems.at[len(shards) + i])
+
+    for i in range(PROJECT_CHUNKS):
+        normed_copy(i).start()
     for copy in copies:
         copy.wait()
 
@@ -164,12 +187,13 @@
     scale = jnp.where(lanes < half, math.log2(math.e) / math.sqrt(head_dim), 1.0).astype(F32)
 
     def project(i, _):
-        rows = pl.ds(pl.multiple_of(i * 256, 256), 256)
+        normed_copy(i).wait()
+        rows = pl.ds(pl.multiple_of(i * chunk, chunk), chunk)
         out = jnp.dot(normed_ref[rows, :width], weight_s[...], preferred_element_type=F32)
         qvk_s[rows, : 3 * half] = (out * scale).astype(BF16)
         return 0
 
-    lax.fori_loop(0, count // 256, project, 0)
+    lax.fori_loop(0, PROJECT_CHUNKS, project, 0)
     lane = lax.broadcasted_iota(jnp.int32, (1, 256), 1)
 
     def span(low):
@@ -244,7 +268,7 @@
             pltpu.VMEM(normed.shape, BF16),
             pltpu.VMEM((width, columns), BF16),
             pltpu.VMEM((count, columns + 64), BF16),
-            pltpu.SemaphoreType.DMA((len(shards) + 1,)),
+            pltpu.SemaphoreType.DMA((len(shards) + PROJECT_CHUNKS,)),
         ],
         compiler_params=params(),
         cost_estimate=cost(10**10, 2**24),
@@ -252,66 +276,63 @@
     )(place, key_windows(segs), segs, normed, *shards)
 
 
-def both_halves(place_ref, own, other):
-    first = jnp.full(own.shape, place_ref[3], jnp.int32) == 0
-    own, other = own.astype(F32), other.astype(F32)
-    halves = [jnp.where(first, own, other), jnp.where(first, other, own)]
-    return jnp.concatenate([part[:, 64:] for part in halves], axis=1).astype(BF16)
-
-
-def pool_kernel(place_ref, rows_mean_ref, own_ref, other_ref, weight_ref, unit_ref, out_ref):
-    context = both_halves(place_ref, own_ref[...], other_ref[...])
-    pooled = rows_mean_ref[...] + join(jnp.dot(context, weight_ref[...], preferred_element_type=F32))
+def pool_kernel(rows_mean_ref, own_ref, other_ref, own_weight_ref, other_weight_ref, unit_ref, out_ref):
+    pooled = rows_mean_ref[...]
+    for context_ref, weight_ref in ((own_ref, own_weight_ref), (other_ref, other_weight_ref)):
+        pooled += join(jnp.dot(context_ref[:, 64:], weight_ref[...], preferred_element_type=F32))
     unit = pooled * lax.rsqrt(jnp.sum(pooled * pooled, axis=1, keepdims=True) + 1e-06)
     unit_ref[...] = unit
     out_ref[...] = jnp.broadcast_to(unit.astype(BF16)[None], out_ref.shape)
 
 
-def pool(place, rows_mean, own, other, rest, copies):
+def pool(rows_mean, own, other, own_weight, other_weight, copies):
     images, width = rows_mean.shape
     last = own.shape[0] // (2 * images) - 1
     tail = pl.BlockSpec((2 * images, own.shape[1]), lambda i: (last, 0))
+    weight = whole(own_weight.shape)
     return pl.pallas_call(
         pool_kernel,
         grid=(1,),
         out_shape=(jax.ShapeDtypeStruct((images, width), F32), jax.ShapeDtypeStruct((copies, images, width), BF16)),
-        in_specs=[SMEM, whole((images, width)), tail, tail, whole((width, width))],
+        in_specs=[whole((images, width)), tail, tail, weight, weight],
         out_specs=(whole((images, width)), whole((copies, images, width))),
         compiler_params=params(),
         cost_estimate=cost(2**25, 2**22),
         name="pool",
-    )(place, rows_mean, own, other, rest)
-
-
-def encode_kernel(place_ref, x_ref, own_ref, other_ref, weight_ref, out_ref):
-    context = both_halves(place_ref, own_ref[...], other_ref[...])
-    attended = jnp.dot(context, weight_ref[...], preferred_element_type=F32)
+    )(rows_mean, own, other, own_weight, other_weight)
+
+
+def encode_kernel(x_ref, own_ref, other_ref, own_weight_ref, other_weight_ref, out_ref, weight_s):
+    depth = own_weight_ref.shape[0] + 64
+
+    @pl.when(pl.program_id(0) == 0)
+    def _():
+        for at, weight_ref in enumerate((own_weight_ref, other_weight_ref)):
+            weight_s[at * depth : at * depth + 64, :] = jnp.zeros((64, weight_s.shape[1]), BF16)
+            weight_s[at * depth + 64 : (at + 1) * depth, :] = weight_ref[...]
+
+    attended = jnp.dot(own_ref[...], weight_s[:depth, :], preferred_element_type=F32)
+    attended += jnp.dot(other_ref[...], weight_s[depth:, :], preferred_element_type=F32)
     out_ref[...] = (x_ref[...].astype(F32) + attended).astype(BF16)
 
 
-def encode(place, x, own, other, rest):
+def encode(x, own, other, own_weight, other_weight):
     count, width = x.shape
-    rows = 256
+    rows = 512
     block = pl.BlockSpec((rows, width), lambda i: (i, 0))
     half = pl.BlockSpec((rows, own.shape[1]), lambda i: (i, 0))
+    weight = whole(own_weight.shape)
     return pl.pallas_call(
         encode_kernel,
         grid=(count // rows,),
         out_shape=jax.ShapeDtypeStruct((count, width), BF16),
-        in_specs=[SMEM, block, half, half, pl.BlockSpec((width, width), lambda i: (0, 0))],
+        in_specs=[block, half, half, weight, weight],
         out_specs=block,
+        scratch_shapes=[pltpu.VMEM((2 * own.shape[1], width), BF16)],
         compiler_params=params(),
         cost_estimate=cost(3 * 10**9, 2**24),
         name="encode",
-    )(place, x, own, other, rest)
-
-
-def text_rows(packed, width):
-    columns = width // 128
-    texts = packed.shape[0] // columns
-    packed = packed.astype(F32).reshape(texts // 8, columns * 8, 128)
-    pieces = [packed[:, at * 8 : at * 8 + 8, :].reshape(texts, 128) for at in range(columns)]
-    return jnp.concatenate(pieces, axis=1)
+    )(x, own, other, own_weight, other_weight)
 
 
 def inverse_norm(values):
@@ -323,68 +344,76 @@
     return -10.0 * sign * jax.nn.sigmoid(-sign * logits)
 
 
-def text_kernel(place_ref, units_ref, text_ref, out_ref):
+def text_kernel(place_ref, units_ref, mine_ref, theirs_ref, out_ref):
     units = units_ref[...]
     images, width = units.shape
-    text = text_rows(text_ref[...], width)
-    texts = text.shape[0]
-    scale = inverse_norm(text)
-    dots = lax.dot_general(text.astype(BF16), units, (((1,), (1,)), ((), ())), preferred_element_type=F32)
-    image = lax.broadcasted_iota(jnp.int32, (texts, images), 1) - place_ref[1] * IMG_DEV
-    index = lax.broadcasted_iota(jnp.int32, (texts, images), 0) - place_ref[2] * IMG_DEV
-    diagonal = (image == index) & (image >= 0) & (image < IMG_DEV)
-    coeffs = sigmoid_coeffs(10.0 * dots * scale - 3.0, diagonal)
-    out_ref[...] = join(jnp.dot(split(coeffs), units, preferred_element_type=F32)).astype(BF16)
-
-
-def text_terms(place, units, rest):
+    owners = mine_ref.shape[0]
+    texts = owners * IMG_DEV
+    row, core = place_ref[1], place_ref[3]
+    for text_ref, at in ((mine_ref, core), (theirs_ref, 1 - core)):
+        text = text_ref[:, row].astype(F32).reshape(texts, width)
+        scale = inverse_norm(text)
+        dots = lax.dot_general(text.astype(BF16), units, (((1,), (1,)), ((), ())), preferred_element_type=F32)
+        image = lax.broadcasted_iota(jnp.int32, (texts, images), 1) - row * IMG_DEV
+        index = lax.broadcasted_iota(jnp.int32, (texts, images), 0)
+        index = index // IMG_DEV * 2 * IMG_DEV + index % IMG_DEV + (at - place_ref[2]) * IMG_DEV
+        diagonal = (image == index) & (image >= 0) & (image < IMG_DEV)
+        coeffs = sigmoid_coeffs(10.0 * dots * scale - 3.0, diagonal)
+        term = join(jnp.dot(split(coeffs), units, preferred_element_type=F32))
+        out_ref[:, at] = term.reshape(owners, IMG_DEV, width).astype(BF16)
+
+
+def text_terms(place, units, mine, theirs):
     images, width = units.shape
-    texts = rest.shape[0] * 128 // width
+    out = (mine.shape[0], 2, IMG_DEV, width)
     return pl.pallas_call(
         text_kernel,
         grid=(1,),
-        out_shape=jax.ShapeDtypeStruct((texts, width), BF16),
-        in_specs=[SMEM, whole((images, width)), pl.BlockSpec((rest.shape[0], 128), lambda i: (0, width // 128))],
-        out_specs=whole((texts, width)),
+        out_shape=jax.ShapeDtypeStruct(out, BF16),
+        in_specs=[SMEM, whole((images, width)), whole(mine.shape), whole(mine.shape)],
+        out_specs=whole(out),
         compiler_params=params(),
         cost_estimate=cost(2**26, 2**21),
         name="text_terms",
-    )(place, units, rest)
-
-
-def image_kernel(place_ref, unit_ref, text_ref, out_ref):
+    )(place, units, mine, theirs)
+
+
+def image_kernel(place_ref, unit_ref, mine_ref, theirs_ref, out_ref):
     unit = unit_ref[...]
     images, width = unit.shape
-    text = text_ref[...]
-    texts = text.shape[0]
-    scale = inverse_norm(text.astype(F32))
-    dots = lax.dot_general(text, split(unit), (((1,), (1,)), ((), ())), preferred_element_type=F32)
-    dots = dots[:, :images] + dots[:, images:]
-    image = lax.broadcasted_iota(jnp.int32, (texts, images), 1) + place_ref[0] * images
-    diagonal = image == lax.broadcasted_iota(jnp.int32, (texts, images), 0)
-    coeffs = sigmoid_coeffs(10.0 * dots * scale - 3.0, diagonal) * scale
-    out_ref[...] = join(jnp.dot(split(coeffs.T), text, preferred_element_type=F32))
-
-
-def image_gradient(place, unit, text):
+    grad = jnp.zeros(unit.shape, F32)
+    for text_ref, low in ((mine_ref, place_ref[0]), (theirs_ref, -1)):
+        text = text_ref[...]
+        texts = text.shape[0]
+        scale = inverse_norm(text.astype(F32))
+        dots = lax.dot_general(text, split(unit), (((1,), (1,)), ((), ())), preferred_element_type=F32)
+        dots = dots[:, :images] + dots[:, images:]
+        image = lax.broadcasted_iota(jnp.int32, (texts, images), 1) + low * images
+        diagonal = image == lax.broadcasted_iota(jnp.int32, (texts, images), 0)
+        coeffs = sigmoid_coeffs(10.0 * dots * scale - 3.0, diagonal) * scale
+        grad += join(jnp.dot(split(coeffs.T), text, preferred_element_type=F32))
+    out_ref[...] = grad
+
+
+def image_gradient(place, unit, mine, theirs):
     return pl.pallas_call(
         image_kernel,
         grid=(1,),
         out_shape=jax.ShapeDtypeStruct(unit.shape, F32),
-        in_specs=[SMEM, whole(unit.shape), whole(text.shape)],
+        in_specs=[SMEM, whole(unit.shape), whole(mine.shape), whole(mine.shape)],
         out_specs=whole(unit.shape),
         compiler_params=params(),
         cost_estimate=cost(2**28, 2**22),
         name="image_gradient",
-    )(place, unit, text)
-
-
-def gather_weights(own, beside):
+    )(place, unit, mine, theirs)
+
+
+def gather_weights(own, first, second):
     up, down, across, beside = lax.optimization_barrier(
-        (take(own, FROM_UP), take(own, FROM_DOWN), take(own, FROM_ACROSS), beside)
+        (take(own, FROM_UP), take(own, FROM_DOWN), take(own, FROM_ACROSS), first())
     )
-    far, across_up, across_down = lax.optimization_barrier(
-        (take(up, FROM_UP), take(up, FROM_ACROSS), take(across, FROM_DOWN))
+    far, across_up, across_down, beside = lax.optimization_barrier(
+        (take(up, FROM_UP), take(up, FROM_ACROSS), take(across, FROM_DOWN), second(beside))
     )
     third = own.shape[0] // 3
     last = [
@@ -416,32 +445,49 @@
     depth = query_weight.shape[0] * 2
     steps = [(0, 0), (1, 0), (-1, 0), (2, 0), (0, 1), (1, 1), (-1, 1), (2, 1)]
     firsts = [((y_at + dy) % SIDE * 2 + (z_hi + dz) % 2) * depth for dy, dz in steps]
-    place = jnp.stack([col_at * n_row + row_at, row_at, col_at, core] + firsts).astype(jnp.int32)
+    place = jnp.stack([col_at // 2 * n_row + row_at, row_at, col_at, core] + firsts).astype(jnp.int32)
     texts = text_embeds.shape[0]
 
-    mine, other, rest, copies = pack(place, query_weight, key_weight, value_weight, out_weight, text_embeds, n_row)
-    rest = lax.all_gather(rest, "col", axis=0, tiled=True)
+    owners = n_col // 2
+    mine, other = pack(place, query_weight, key_weight, value_weight)
     theirs = take(other, FROM_CORE)
     other_segs = take(segment_ids, FROM_CORE)
     own = jnp.where(core == 0, jnp.concatenate([mine, theirs]), jnp.concatenate([theirs, mine]))
-    own, rows, other_segs, copies = lax.optimization_barrier((own, patch_rows, other_segs, copies))
-    normed, rows_mean = norm(rows, norm_gain, segment_ids)
-    column_text = lax.all_to_all(copies, "row", 0, 0)
-    shards, (normed, column_text) = gather_weights(own, (normed, column_text))
-    every_text = lax.all_gather(column_text.reshape(n_row * texts, width), "col", axis=0, tiled=True)
-    other_normed = take(normed, FROM_CORE)
+    own, rows, other_segs, out_rows, own_text = lax.optimization_barrier(
+        (own, patch_rows, other_segs, out_weight, text_embeds)
+    )
+
+    def first():
+        column_text = lax.all_to_all(copies_of(own_text, n_row), "row", 0, 0)
+        return norm(rows, norm_gain, segment_ids), column_text
+
+    def second(beside):
+        (normed, rows_mean), column_text = beside
+        text_copies = copies_of(column_text.reshape(n_row * texts, width), owners)
+        return normed, take(normed, FROM_CORE), rows_mean, text_copies, copies_of(out_rows, owners)
+
+    shards, beside = gather_weights(own, first, second)
+    normed, other_normed, rows_mean, text_copies, out_copies = beside
+    own_out = lax.all_to_all(out_copies, "col", 0, 0, axis_index_groups=SAME_CORE)
     for_other = attend(place, other_segs, other_normed, shards)
+    for_other, own_out = lax.optimization_barrier((for_other, own_out))
     context_other = take(for_other, FROM_CORE)
+    own_out = own_out.reshape(width // 2, width)
+    other_out = take(own_out, FROM_CORE)
+    own_text = lax.all_to_all(text_copies, "col", 0, 0, axis_index_groups=SAME_CORE)
+    own_text = own_text.reshape(owners, n_row, texts, width)
     context_own = attend(place, segment_ids, normed, shards)
-    context_own, rest = lax.optimization_barrier((context_own, rest))
-    unit, units = pool(place, rows_mean, context_own, context_other, rest, n_row)
+    unit, units = pool(rows_mean, context_own, context_other, own_out, other_out, n_row)
+    units, own_text = lax.optimization_barrier((units, own_text))
+    other_text = take(own_text, FROM_CORE)
     units = lax.all_to_all(units, "row", 0, 0)
-    encoded = encode(place, patch_rows, context_own, context_other, rest)
+    encoded = encode(patch_rows, context_own, context_other, own_out, other_out)
     units, encoded = lax.optimization_barrier((units, encoded))
-    terms = text_terms(place, units.reshape(n_row * IMG_DEV, width), rest)
-    terms, unit, every_text = lax.optimization_barrier((terms, unit, every_text))
+    terms = text_terms(place, units.reshape(n_row * IMG_DEV, width), own_text, other_text)
+    terms, unit = lax.optimization_barrier((terms, unit))
     terms = lax.all_to_all(terms.reshape(n_col, texts, width), "col", 0, 0)
-    image_grad = image_gradient(place, unit, every_text)
+    every = owners * n_row * texts
+    image_grad = image_gradient(place, unit, own_text.reshape(every, width), other_text.reshape(every, width))
     return (encoded, image_grad, jnp.sum(terms.astype(F32), axis=0))
 
 

time: 156 us -> 142 us (0.910)
  waiting for transfers between devices: 29.5 us -> 14.5 us
  between operations: 14.4 us -> 1.06 us
  starting transfers between devices: 38.4 us -> 47.1 us
  Pallas kernels: 63.5 us -> 70.7 us
    ppermute x13 -> x15, waiting for transfers between devices: 24.4 us -> 9.72 us  [take(): return lax.ppermute(values, AXES, found)]
    all_to_all x1 -> x3, starting transfers between devices: 4.02 us -> 13.4 us  [the longest x1 5.47 us: body(): lax.all_to_all(text_copies, 'col', 0, 0, axis_index_groups=SAME_CORE)]
    pallas_call x2 -> x5, Pallas kernels: 4.58 us -> 11 us  [the longest x3 5.59 us: copies_of(): pl.pallas_call(copies_kernel, grid=(1,), out_shape=jax.ShapeDtypeStruct(o...]
    ppermute x13 -> x15, starting transfers between devices: 24.1 us -> 20.6 us  [take(): return lax.ppermute(values, AXES, found)]
    all_to_all x1, starting transfers between devices: 6.17 us -> 8.16 us  [body(): terms = lax.all_to_all(terms.reshape(n_col, texts, width), 'col', 0, 0)]
    unnamed x37 -> x35, local copies, waits for them, and re-layouts: 3.26 us -> 1.99 us
  transfers between devices with their start and end apart: 18 -> 20, of which waited for: 7 -> 6; matrix products, arithmetic and copies ran while one was open for 4% -> 4% of each run, Pallas kernels for 39% -> 46%
where the time goes in v3:
time: 142 us
  Pallas kernels  70.7 us (50%)
  starting transfers between devices  47.1 us (33%)
  waiting for transfers between devices  14.5 us (10%)
  other arithmetic  4.76 us (3%)
  local copies, waits for them, and re-layouts  3.39 us (2%)
    pallas_call x2, Pallas kernels, attend(): pl.pallas_call(attend_kernel, grid=(1,), out_shape=jax.ShapeDtypeStruct((...  38.6 us
    ppermute x15, starting transfers between devices, take(): return lax.ppermute(values, AXES, found)  20.6 us
    ppermute x15, waiting for transfers between devices, take(): return lax.ppermute(values, AXES, found)  9.72 us
    all_to_all x1, starting transfers between devices, body(): terms = lax.all_to_all(terms.reshape(n_col, texts, width), 'col', 0, 0)  8.16 us
    pallas_call x1, Pallas kernels, encode(): pl.pallas_call(encode_kernel, grid=(count // rows,), out_shape=jax.ShapeD...  8.03 us
    pallas_call x3, Pallas kernels, copies_of(): pl.pallas_call(copies_kernel, grid=(1,), out_shape=jax.ShapeDtypeStruct(o...  5.59 us
    pallas_call x1, Pallas kernels, norm(): pl.pallas_call(norm_kernel, grid=(1,), out_shape=(jax.ShapeDtypeStruct((c...  5.48 us
    all_to_all x1, starting transfers between devices, body(): lax.all_to_all(text_copies, 'col', 0, 0, axis_index_groups=SAME_CORE)  5.47 us
  transfers between devices with their start and end apart: 20, of which 6 were waited for; matrix products, arithmetic and copies ran while one was open for 4% of the time, Pallas kernels for 46%

profile of v3, /device:TPU:1, one launch (start us, length us, event | category | flops | bytes accessed | tf_op | source)
XLA Modules:
  0.0 141.5 jit_solution(7553231713968544395)
XLA Ops:
  1.4 2.3 %pack.1 = (bf16[72,1728]{1,0:T(8,128)(2,1)}, bf16[72,1728]{1,0:T(8,128)(2,1)}) custom-call(s32[12]{0:T(128)} %stack.61.place_ref, bf16[72,1152]{1,0:T(8,128)(2,1)} %q_ref.1, bf16[72,1152]{1,0:T(8,128)(2,1)} %k_ref.1, bf16[72,1152]{1,0:T(8,128)(2,1)} %v_ref.1), custom_call_target="tpu_custom_call" | custom-call | bytes 2097152 | tf_op jit(solution)/shard_map/pack/pallas_call | solution.py:79
  7.7 2.9 %collective-permute-start.2 = (bf16[144,1728]{1,0:T(8,128)(2,1)S(1)}, bf16[144,1728]{1,0:T(8,128)(2,1)S(1)}, u32[]{:S(2)}, u32[]{:S(2)}) collective-permute-start(bf16[144,1728]{1,0:T(8,128)(2,1)S(1)} %maximum_select_fusion.refs_0_), channel_id=1, source_target_pairs={{4,0},{5,1},{20,16},{21,17},{6,2},{7,3},{22,18},{23,19},{8,4},{9,5... | collective-permute-start | bytes 1493000 | tf_op jit(solution)/shard_map/ppermute | solution.py:59
  10.6 3.8 %collective-permute-start.4 = (bf16[144,1728]{1,0:T(8,128)(2,1)S(1)}, bf16[144,1728]{1,0:T(8,128)(2,1)S(1)}, u32[]{:S(2)}, u32[]{:S(2)}) collective-permute-start(bf16[144,1728]{1,0:T(8,128)(2,1)S(1)} %maximum_select_fusion.refs_0_), channel_id=1, source_target_pairs={{18,0},{19,1},{2,16},{3,17},{16,2},{17,3},{0,18},{1,19},{22,4},{23... | collective-permute-start | bytes 1493000 | tf_op jit(solution)/shard_map/ppermute | solution.py:59
  15.8 4.2 %all-to-all-start = ((bf16[8,8,1152]{2,1,0:T(8,128)(2,1)}), bf16[8,8,1152]{2,1,0:T(8,128)(2,1)S(1)}, u32[]{:S(2)}, u32[]{:S(2)}) async-start(bf16[8,8,1152]{2,1,0:T(8,128)(2,1)} %copies.3), calls=%async_computation | async-start | bytes 294912 | tf_op jit(solution)/shard_map/all_to_all | solution.py:461
  20.5 5.5 %norm.1 = (bf16[1024,1280]{1,0:T(8,128)(2,1)}, f32[8,1152]{1,0:T(8,128)}) custom-call(bf16[1024,1152]{1,0:T(8,128)(2,1)} %x_ref.2, f32[1,1152]{1,0:T(1,128)} %reshape.256.gain_ref, s32[1,1024]{1,0:T(1,128)} %segs_ref.3), custom_call_target="tpu_custom_call" | custom-call | bytes 16777216 | tf_op jit(solution)/shard_map/norm/pallas_call | solution.py:131
  26.1 1.6 %collective-permute-start.8 = (bf16[1024,1280]{1,0:T(8,128)(2,1)}, bf16[1024,1280]{1,0:T(8,128)(2,1)}, u32[]{:S(2)}, u32[]{:S(2)}) collective-permute-start(bf16[1024,1280]{1,0:T(8,128)(2,1)} %get-tuple-element.50.normed_hbm), channel_id=1, source_target_pairs={{1,0},{0,1},{17,16},{16,17},{3,2},{2,3},{19,18},{18,19},{5,4},{4,5... | collective-permute-start | bytes 7864328 | tf_op jit(solution)/shard_map/ppermute | solution.py:59
  28.9 3.0 %collective-permute-start.5 = (bf16[144,1728]{1,0:T(8,128)(2,1)S(1)}, bf16[144,1728]{1,0:T(8,128)(2,1)S(1)}, u32[]{:S(2)}, u32[]{:S(2)}) collective-permute-start(bf16[144,1728]{1,0:T(8,128)(2,1)S(1)} %collective-permute-done.2.refs_1_), channel_id=1, source_target_pairs={{4,0},{5,1},{20,16},{21,17},{6,2},{7,3},{22,18},{23,19},{8,4},{9,5... | collective-permute-start | bytes 1493000 | tf_op jit(solution)/shard_map/ppermute | solution.py:59
  31.9 1.7 %collective-permute-start.6 = (bf16[144,1728]{1,0:T(8,128)(2,1)S(1)}, bf16[144,1728]{1,0:T(8,128)(2,1)S(1)}, u32[]{:S(2)}, u32[]{:S(2)}) collective-permute-start(bf16[144,1728]{1,0:T(8,128)(2,1)S(1)} %collective-permute-done.2.refs_1_), channel_id=1, source_target_pairs={{18,0},{19,1},{2,16},{3,17},{16,2},{17,3},{0,18},{1,19},{22,4},{23... | collective-permute-start | bytes 1493000 | tf_op jit(solution)/shard_map/ppermute | solution.py:59
  33.9 2.1 %copies.5 = bf16[8,72,1152]{2,1,0:T(8,128)(2,1)} custom-call(bf16[72,1152]{1,0:T(8,128)(2,1)} %in_ref.1), custom_call_target="tpu_custom_call" | custom-call | bytes 4194304 | tf_op jit(solution)/shard_map/copies/pallas_call | solution.py:97
  37.2 2.1 %copies.4 = bf16[8,64,1152]{2,1,0:T(8,128)(2,1)} custom-call(bf16[64,1152]{1,0:T(8,128)(2,1)} %bitcast.74), custom_call_target="tpu_custom_call" | custom-call | bytes 4194304 | tf_op jit(solution)/shard_map/copies/pallas_call | solution.py:97
  39.3 3.6 %collective-permute-done.5.refs_3_ = bf16[144,1728]{1,0:T(8,128)(2,1)S(1)} collective-permute-done((bf16[144,1728]{1,0:T(8,128)(2,1)S(1)}, bf16[144,1728]{1,0:T(8,128)(2,1)S(1)}, u32[]{:S(2)}, u32[]{:S(2)}) %collective-permute-start.5) | collective-permute-done | bytes 497696 | tf_op jit(solution)/shard_map/ppermute | solution.py:59
  42.9 3.1 %collective-permute-done.6.refs_5_ = bf16[144,1728]{1,0:T(8,128)(2,1)S(1)} collective-permute-done((bf16[144,1728]{1,0:T(8,128)(2,1)S(1)}, bf16[144,1728]{1,0:T(8,128)(2,1)S(1)}, u32[]{:S(2)}, u32[]{:S(2)}) %collective-permute-start.6) | collective-permute-done | bytes 497696 | tf_op jit(solution)/shard_map/ppermute | solution.py:59
  50.1 3.8 %all-to-all-start.1 = ((bf16[8,72,1152]{2,1,0:T(8,128)(2,1)}), bf16[8,72,1152]{2,1,0:T(8,128)(2,1)S(1)}, u32[]{:S(2)}, u32[]{:S(2)}) async-start(bf16[8,72,1152]{2,1,0:T(8,128)(2,1)} %copies.5), calls=%async_computation.1 | async-start | bytes 2654208 | tf_op jit(solution)/shard_map/all_to_all | solution.py:471
  54.6 19.2 %attend.3 = bf16[1040,640]{1,0:T(8,128)(2,1)} custom-call(s32[12]{0:T(128)} %stack.61.place_ref, s32[2,4]{1,0:T(2,128)} %pad_add_fusion.1.window_ref, s32[1,1024]{1,0:T(1,128)} %copy-done.10, bf16[1024,1280]{1,0:T(8,128)(2,1)} %collective-permute-done.8.normed_hbm, bf16[144,1728]{1,0:T(8,128)(2,1)} %copy-done.5, bf16[144,1728]{1,0:T(8,128)(2,1)} %copy-done.12, ...), custom_call_target="tpu_custom_call" | custom-call | flops 10000000000 | bytes 16777216 | tf_op jit(solution)/shard_map/attend/pallas_call | solution.py:261
  73.8 3.0 %collective-permute-start.12 = (bf16[1040,640]{1,0:T(8,128)(2,1)}, bf16[1040,640]{1,0:T(8,128)(2,1)}, u32[]{:S(2)}, u32[]{:S(2)}) collective-permute-start(bf16[1040,640]{1,0:T(8,128)(2,1)} %attend.3), channel_id=1, source_target_pairs={{1,0},{0,1},{17,16},{16,17},{3,2},{2,3},{19,18},{18,19},{5,4},{4,5... | collective-permute-start | bytes 3993608 | tf_op jit(solution)/shard_map/ppermute | solution.py:59
  77.1 5.5 %all-to-all-start.2 = ((bf16[8,64,1152]{2,1,0:T(8,128)(2,1)}), bf16[8,64,1152]{2,1,0:T(8,128)(2,1)S(1)}, u32[]{:S(2)}, u32[]{:S(2)}) async-start(bf16[8,64,1152]{2,1,0:T(8,128)(2,1)} %copies.4), calls=%async_computation.2 | async-start | bytes 2359296 | tf_op jit(solution)/shard_map/all_to_all | solution.py:477
  83.1 19.4 %attend.2.own_ref = bf16[1040,640]{1,0:T(8,128)(2,1)} custom-call(s32[12]{0:T(128)} %stack.61.place_ref, s32[2,4]{1,0:T(2,128)} %pad_add_fusion.window_ref, s32[1,1024]{1,0:T(1,128)} %segs_ref.3, bf16[1024,1280]{1,0:T(8,128)(2,1)} %get-tuple-element.50.normed_hbm, bf16[144,1728]{1,0:T(8,128)(2,1)} %copy-done.5, bf16[144,1728]{1,0:T(8,128)(2,1)} %copy-done.12, ...), custom_call_target="tpu_custom_call" | custom-call | flops 10000000000 | bytes 16777216 | tf_op jit(solution)/shard_map/attend/pallas_call | solution.py:261
  102.6 3.1 %pool.1 = (f32[8,1152]{1,0:T(8,128)}, bf16[8,8,1152]{2,1,0:T(8,128)(2,1)}) custom-call(f32[8,1152]{1,0:T(8,128)} %get-tuple-element.49.rows_mean_ref, bf16[1040,640]{1,0:T(8,128)(2,1)} %attend.2.own_ref, bf16[1040,640]{1,0:T(8,128)(2,1)} %collective-permute-done.12.other_ref, bf16[576,1152]{1,0:T(8,128)(2,1)} %bitcast.69, ...), custom_call_target="tpu_custom_call" | custom-call | flops 33554432 | bytes 4194304 | tf_op jit(solution)/shard_map/pool/pallas_call | solution.py:293
  106.2 5.0 %all-to-all-start.3 = ((bf16[8,8,1152]{2,1,0:T(8,128)(2,1)}), bf16[8,8,1152]{2,1,0:T(8,128)(2,1)S(1)}, u32[]{:S(2)}, u32[]{:S(2)}) async-start(bf16[8,8,1152]{2,1,0:T(8,128)(2,1)} %get-tuple-element.62), calls=%async_computation.3 | async-start | bytes 294912 | tf_op jit(solution)/shard_map/all_to_all | solution.py:483
  111.2 8.0 %encode.1 = bf16[1024,1152]{1,0:T(8,128)(2,1)} custom-call(bf16[1024,1152]{1,0:T(8,128)(2,1)} %x_ref.2, bf16[1040,640]{1,0:T(8,128)(2,1)} %attend.2.own_ref, bf16[1040,640]{1,0:T(8,128)(2,1)} %collective-permute-done.12.other_ref, bf16[576,1152]{1,0:T(8,128)(2,1)} %bitcast.70, bf16[576,1152]{1,0:T(8,128)(2,1)} %collective-permute-done.13.other_weight_ref), custom_call_target="tpu_custom_call" | custom-call | flops 3000000000 | bytes 16777216 | tf_op jit(solution)/shard_map/encode/pallas_call | solution.py:325
  120.3 3.1 %text_terms.1 = bf16[8,2,8,1152]{3,2,1,0:T(8,128)(2,1)} custom-call(s32[12]{0:T(128)} %stack.61.place_ref, bf16[64,1152]{1,0:T(8,128)(2,1)} %bitcast.73, bf16[8,8,8,1152]{3,2,1,0:T(8,128)(2,1)} %bitcast.66, bf16[8,8,8,1152]{3,2,1,0:T(8,128)(2,1)} %copy-done.2), custom_call_target="tpu_custom_call" | custom-call | flops 67108864 | bytes 2097152 | tf_op jit(solution)/shard_map/text_terms/pallas_call | solution.py:369
  123.5 8.2 %all-to-all-start.4 = ((bf16[16,8,1152]{2,1,0:T(8,128)(2,1)}), bf16[16,8,1152]{2,1,0:T(8,128)(2,1)S(1)}, u32[]{:S(2)}, u32[]{:S(2)}) async-start(bf16[16,8,1152]{2,1,0:T(8,128)(2,1)} %bitcast.72), calls=%async_computation.4 | async-start | bytes 589824 | tf_op jit(solution)/shard_map/all_to_all | solution.py:488
  131.6 4.5 %image_gradient.1 = f32[8,1152]{1,0:T(8,128)} custom-call(s32[12]{0:T(128)} %stack.61.place_ref, f32[8,1152]{1,0:T(8,128)} %get-tuple-element.67.unit_ref, bf16[512,1152]{1,0:T(8,128)(2,1)} %bitcast.67, bf16[512,1152]{1,0:T(8,128)(2,1)} %bitcast.71), custom_call_target="tpu_custom_call" | custom-call | flops 268435456 | bytes 4194304 | tf_op jit(solution)/shard_map/image_gradient/pallas_call | solution.py:399
  136.1 4.7 %all-to-all-done.4 = bf16[16,8,1152]{2,1,0:T(8,128)(2,1)S(1)} async-done(((bf16[16,8,1152]{2,1,0:T(8,128)(2,1)}), bf16[16,8,1152]{2,1,0:T(8,128)(2,1)S(1)}, u32[]{:S(2)}, u32[]{:S(2)}) %all-to-all-start.4) | async-done | bytes 294944 | tf_op jit(solution)/shard_map/all_to_all | solution.py:488
  (81 shorter events, 17.2 us)
Async XLA Ops:
  0.6 19.3 %copy-start.11 = (f32[1152]{0:T(1024)S(1)}, f32[1152]{0:T(1024)}, u32[]{:S(2)}) copy-start(f32[1152]{0:T(1024)} %param.10) | copy-start | bytes 13828
  3.7 2.8 %collective-permute-start = (bf16[72,1728]{1,0:T(8,128)(2,1)}, bf16[72,1728]{1,0:T(8,128)(2,1)S(1)}, u32[]{:S(2)}, u32[]{:S(2)}) collective-permute-start(bf16[72,1728]{1,0:T(8,128)(2,1)} %get-tuple-element.37), channel_id=1, source_target_pairs={{1,0},{0,1},{17,16},{16,17},{3,2},{2,3},{19,18},{18,19},{5,4},{4,5... | collective-permute-start | bytes 746504 | tf_op jit(solution)/shard_map/ppermute | solution.py:59
  5.1 2.6 %collective-permute-start.1 = (s32[1,1024]{1,0:T(1,128)}, s32[1,1024]{1,0:T(1,128)S(1)}, u32[]{:S(2)}, u32[]{:S(2)}) collective-permute-start(s32[1,1024]{1,0:T(1,128)} %segs_ref.3), channel_id=1, source_target_pairs={{1,0},{0,1},{17,16},{16,17},{3,2},{2,3},{19,18},{18,19},{5,4},{4,5... | collective-permute-start | bytes 12296 | tf_op jit(solution)/shard_map/ppermute | solution.py:59
  7.7 18.3 %copy-start.5 = (bf16[144,1728]{1,0:T(8,128)(2,1)}, bf16[144,1728]{1,0:T(8,128)(2,1)S(1)}, u32[]{:S(2)}) copy-start(bf16[144,1728]{1,0:T(8,128)(2,1)S(1)} %maximum_select_fusion.refs_0_) | copy-start | bytes 1492996
  7.7 29.3 %copy-start.10 = (s32[1,1024]{1,0:T(1,128)}, s32[1,1024]{1,0:T(1,128)S(1)}, u32[]{:S(2)}) copy-start(s32[1,1024]{1,0:T(1,128)S(1)} %collective-permute-done.1.segs_ref) | copy-start | bytes 12292
  7.7 18.3 %collective-permute-start.2 = (bf16[144,1728]{1,0:T(8,128)(2,1)S(1)}, bf16[144,1728]{1,0:T(8,128)(2,1)S(1)}, u32[]{:S(2)}, u32[]{:S(2)}) collective-permute-start(bf16[144,1728]{1,0:T(8,128)(2,1)S(1)} %maximum_select_fusion.refs_0_), channel_id=1, source_target_pairs={{4,0},{5,1},{20,16},{21,17},{6,2},{7,3},{22,18},{23,19},{8,4},{9,5... | collective-permute-start | bytes 1493000 | tf_op jit(solution)/shard_map/ppermute | solution.py:59
  10.6 15.4 %collective-permute-start.3 = (bf16[144,1728]{1,0:T(8,128)(2,1)S(1)}, bf16[144,1728]{1,0:T(8,128)(2,1)S(1)}, u32[]{:S(2)}, u32[]{:S(2)}) collective-permute-start(bf16[144,1728]{1,0:T(8,128)(2,1)S(1)} %maximum_select_fusion.refs_0_), channel_id=1, source_target_pairs={{12,0},{13,1},{28,16},{29,17},{14,2},{15,3},{30,18},{31,19},{0,4},... | collective-permute-start | bytes 1493000 | tf_op jit(solution)/shard_map/ppermute | solution.py:59
  10.6 15.5 %collective-permute-start.4 = (bf16[144,1728]{1,0:T(8,128)(2,1)S(1)}, bf16[144,1728]{1,0:T(8,128)(2,1)S(1)}, u32[]{:S(2)}, u32[]{:S(2)}) collective-permute-start(bf16[144,1728]{1,0:T(8,128)(2,1)S(1)} %maximum_select_fusion.refs_0_), channel_id=1, source_target_pairs={{18,0},{19,1},{2,16},{3,17},{16,2},{17,3},{0,18},{1,19},{22,4},{23... | collective-permute-start | bytes 1493000 | tf_op jit(solution)/shard_map/ppermute | solution.py:59
  15.8 10.2 %all-to-all-start = ((bf16[8,8,1152]{2,1,0:T(8,128)(2,1)}), bf16[8,8,1152]{2,1,0:T(8,128)(2,1)S(1)}, u32[]{:S(2)}, u32[]{:S(2)}) async-start(bf16[8,8,1152]{2,1,0:T(8,128)(2,1)} %copies.3), calls=%async_computation | async-start | bytes 294912 | tf_op jit(solution)/shard_map/all_to_all | solution.py:461
  26.1 21.5 %collective-permute-start.8 = (bf16[1024,1280]{1,0:T(8,128)(2,1)}, bf16[1024,1280]{1,0:T(8,128)(2,1)}, u32[]{:S(2)}, u32[]{:S(2)}) collective-permute-start(bf16[1024,1280]{1,0:T(8,128)(2,1)} %get-tuple-element.50.normed_hbm), channel_id=1, source_target_pairs={{1,0},{0,1},{17,16},{16,17},{3,2},{2,3},{19,18},{18,19},{5,4},{4,5... | collective-permute-start | bytes 7864328 | tf_op jit(solution)/shard_map/ppermute | solution.py:59
  28.9 14.0 %collective-permute-start.5 = (bf16[144,1728]{1,0:T(8,128)(2,1)S(1)}, bf16[144,1728]{1,0:T(8,128)(2,1)S(1)}, u32[]{:S(2)}, u32[]{:S(2)}) collective-permute-start(bf16[144,1728]{1,0:T(8,128)(2,1)S(1)} %collective-permute-done.2.refs_1_), channel_id=1, source_target_pairs={{4,0},{5,1},{20,16},{21,17},{6,2},{7,3},{22,18},{23,19},{8,4},{9,5... | collective-permute-start | bytes 1493000 | tf_op jit(solution)/shard_map/ppermute | solution.py:59
  31.9 14.1 %collective-permute-start.6 = (bf16[144,1728]{1,0:T(8,128)(2,1)S(1)}, bf16[144,1728]{1,0:T(8,128)(2,1)S(1)}, u32[]{:S(2)}, u32[]{:S(2)}) collective-permute-start(bf16[144,1728]{1,0:T(8,128)(2,1)S(1)} %collective-permute-done.2.refs_1_), channel_id=1, source_target_pairs={{18,0},{19,1},{2,16},{3,17},{16,2},{17,3},{0,18},{1,19},{22,4},{23... | collective-permute-start | bytes 1493000 | tf_op jit(solution)/shard_map/ppermute | solution.py:59
  33.7 13.9 %collective-permute-start.7 = (bf16[144,1728]{1,0:T(8,128)(2,1)S(1)}, bf16[144,1728]{1,0:T(8,128)(2,1)S(1)}, u32[]{:S(2)}, u32[]{:S(2)}) collective-permute-start(bf16[144,1728]{1,0:T(8,128)(2,1)S(1)} %collective-permute-done.4.refs_4_), channel_id=1, source_target_pairs={{12,0},{13,1},{28,16},{29,17},{14,2},{15,3},{30,18},{31,19},{0,4},... | collective-permute-start | bytes 1493000 | tf_op jit(solution)/shard_map/ppermute | solution.py:59
  47.6 6.9 %collective-permute-start.9 = (bf16[48,1728]{1,0:T(8,128)(2,1)S(1)}, bf16[48,1728]{1,0:T(8,128)(2,1)}, u32[]{:S(2)}, u32[]{:S(2)}) collective-permute-start(bf16[48,1728]{1,0:T(8,128)(2,1)S(1)} %slice.23), channel_id=1, source_target_pairs={{18,0},{19,1},{2,16},{3,17},{16,2},{17,3},{0,18},{1,19},{22,4},{23... | collective-permute-start | bytes 497672 | tf_op jit(solution)/shard_map/ppermute | solution.py:59
  48.5 6.0 %collective-permute-start.10 = (bf16[48,1728]{1,0:T(8,128)(2,1)S(1)}, bf16[48,1728]{1,0:T(8,128)(2,1)}, u32[]{:S(2)}, u32[]{:S(2)}) collective-permute-start(bf16[48,1728]{1,0:T(8,128)(2,1)S(1)} %slice.24), channel_id=1, source_target_pairs={{4,0},{5,1},{20,16},{21,17},{6,2},{7,3},{22,18},{23,19},{8,4},{9,5... | collective-permute-start | bytes 497672 | tf_op jit(solution)/shard_map/ppermute | solution.py:59
  48.6 5.9 %collective-permute-start.11 = (bf16[48,1728]{1,0:T(8,128)(2,1)S(1)}, bf16[48,1728]{1,0:T(8,128)(2,1)}, u32[]{:S(2)}, u32[]{:S(2)}) collective-permute-start(bf16[48,1728]{1,0:T(8,128)(2,1)S(1)} %slice.25), channel_id=1, source_target_pairs={{12,0},{13,1},{28,16},{29,17},{14,2},{15,3},{30,18},{31,19},{0,4},... | collective-permute-start | bytes 497672 | tf_op jit(solution)/shard_map/ppermute | solution.py:59
  50.1 23.6 %all-to-all-start.1 = ((bf16[8,72,1152]{2,1,0:T(8,128)(2,1)}), bf16[8,72,1152]{2,1,0:T(8,128)(2,1)S(1)}, u32[]{:S(2)}, u32[]{:S(2)}) async-start(bf16[8,72,1152]{2,1,0:T(8,128)(2,1)} %copies.5), calls=%async_computation.1 | async-start | bytes 2654208 | tf_op jit(solution)/shard_map/all_to_all | solution.py:471
  73.8 28.7 %copy-start.1 = (bf16[8,72,1152]{2,1,0:T(8,128)(2,1)}, bf16[8,72,1152]{2,1,0:T(8,128)(2,1)S(1)}, u32[]{:S(2)}) copy-start(bf16[8,72,1152]{2,1,0:T(8,128)(2,1)S(1)} %all-to-all-done.1) | copy-start | bytes 3981316
  73.8 28.7 %collective-permute-start.12 = (bf16[1040,640]{1,0:T(8,128)(2,1)}, bf16[1040,640]{1,0:T(8,128)(2,1)}, u32[]{:S(2)}, u32[]{:S(2)}) collective-permute-start(bf16[1040,640]{1,0:T(8,128)(2,1)} %attend.3), channel_id=1, source_target_pairs={{1,0},{0,1},{17,16},{16,17},{3,2},{2,3},{19,18},{18,19},{5,4},{4,5... | collective-permute-start | bytes 3993608 | tf_op jit(solution)/shard_map/ppermute | solution.py:59
  76.8 25.8 %collective-permute-start.13 = (bf16[576,1152]{1,0:T(8,128)(2,1)S(1)}, bf16[576,1152]{1,0:T(8,128)(2,1)}, u32[]{:S(2)}, u32[]{:S(2)}) collective-permute-start(bf16[576,1152]{1,0:T(8,128)(2,1)S(1)} %bitcast.68), channel_id=1, source_target_pairs={{1,0},{0,1},{17,16},{16,17},{3,2},{2,3},{19,18},{18,19},{5,4},{4,5... | collective-permute-start | bytes 3981320 | tf_op jit(solution)/shard_map/ppermute | solution.py:59
  77.1 28.5 %all-to-all-start.2 = ((bf16[8,64,1152]{2,1,0:T(8,128)(2,1)}), bf16[8,64,1152]{2,1,0:T(8,128)(2,1)S(1)}, u32[]{:S(2)}, u32[]{:S(2)}) async-start(bf16[8,64,1152]{2,1,0:T(8,128)(2,1)} %copies.4), calls=%async_computation.2 | async-start | bytes 2359296 | tf_op jit(solution)/shard_map/all_to_all | solution.py:477
  105.6 13.6 %collective-permute-start.14 = (bf16[8,8,8,1152]{3,2,1,0:T(8,128)(2,1)S(1)}, bf16[8,8,8,1152]{3,2,1,0:T(8,128)(2,1)S(1)}, u32[]{:S(2)}, u32[]{:S(2)}) collective-permute-start(bf16[8,8,8,1152]{3,2,1,0:T(8,128)(2,1)S(1)} %bitcast.65), channel_id=1, source_target_pairs={{1,0},{0,1},{17,16},{16,17},{3,2},{2,3},{19,18},{18,19},{5,4},{4,5... | collective-permute-start | bytes 3538952 | tf_op jit(solution)/shard_map/ppermute | solution.py:59
  106.2 13.0 %all-to-all-start.3 = ((bf16[8,8,1152]{2,1,0:T(8,128)(2,1)}), bf16[8,8,1152]{2,1,0:T(8,128)(2,1)S(1)}, u32[]{:S(2)}, u32[]{:S(2)}) async-start(bf16[8,8,1152]{2,1,0:T(8,128)(2,1)} %get-tuple-element.62), calls=%async_computation.3 | async-start | bytes 294912 | tf_op jit(solution)/shard_map/all_to_all | solution.py:483
  123.5 17.4 %all-to-all-start.4 = ((bf16[16,8,1152]{2,1,0:T(8,128)(2,1)}), bf16[16,8,1152]{2,1,0:T(8,128)(2,1)S(1)}, u32[]{:S(2)}, u32[]{:S(2)}) async-start(bf16[16,8,1152]{2,1,0:T(8,128)(2,1)} %bitcast.72), calls=%async_computation.4 | async-start | bytes 589824 | tf_op jit(solution)/shard_map/all_to_all | solution.py:488
  (11 other events, 82.2 us)

commit v4 on v3

--- a/solution.py
+++ b/solution.py
@@ -26,8 +26,8 @@
     return pl.BlockSpec(shape, lambda i: (0,) * len(shape), pipeline_mode=pl.Buffered(1))
 
 
-def params():
-    return pltpu.CompilerParams(vmem_limit_bytes=60 * 2**20)
+def params(mebibytes=60):
+    return pltpu.CompilerParams(vmem_limit_bytes=mebibytes * 2**20)
 
 
 def cost(flops, bytes_accessed):
@@ -253,7 +253,7 @@
     return jnp.stack([first, (end + KEY_ROWS - 1) // KEY_ROWS - first])
 
 
-def attend(place, segs, normed, shards):
+def attend(place, window, segs, normed, shards):
     count = normed.shape[0]
     width = normed.shape[1] - 128
     columns = width // 2 * 3
@@ -273,7 +273,7 @@
         compiler_params=params(),
         cost_estimate=cost(10**10, 2**24),
         name="attend",
-    )(place, key_windows(segs), segs, normed, *shards)
+    )(place, window, segs, normed, *shards)
 
 
 def pool_kernel(rows_mean_ref, own_ref, other_ref, own_weight_ref, other_weight_ref, unit_ref, out_ref):
@@ -303,7 +303,7 @@
 
 
 def encode_kernel(x_ref, own_ref, other_ref, own_weight_ref, other_weight_ref, out_ref, weight_s):
-    depth = own_weight_ref.shape[0] + 64
+    depth = own_ref.shape[1]
 
     @pl.when(pl.program_id(0) == 0)
     def _():
@@ -311,8 +311,8 @@
             weight_s[at * depth : at * depth + 64, :] = jnp.zeros((64, weight_s.shape[1]), BF16)
             weight_s[at * depth + 64 : (at + 1) * depth, :] = weight_ref[...]
 
-    attended = jnp.dot(own_ref[...], weight_s[:depth, :], preferred_element_type=F32)
-    attended += jnp.dot(other_ref[...], weight_s[depth:, :], preferred_element_type=F32)
+    context = jnp.concatenate([own_ref[...], other_ref[...]], axis=1)
+    attended = jnp.dot(context, weight_s[...], preferred_element_type=F32)
     out_ref[...] = (x_ref[...].astype(F32) + attended).astype(BF16)
 
 
@@ -372,7 +372,7 @@
         out_shape=jax.ShapeDtypeStruct(out, BF16),
         in_specs=[SMEM, whole((images, width)), whole(mine.shape), whole(mine.shape)],
         out_specs=whole(out),
-        compiler_params=params(),
+        compiler_params=params(40),
         cost_estimate=cost(2**26, 2**21),
         name="text_terms",
     )(place, units, mine, theirs)
@@ -464,19 +464,20 @@
     def second(beside):
         (normed, rows_mean), column_text = beside
         text_copies = copies_of(column_text.reshape(n_row * texts, width), owners)
-        return normed, take(normed, FROM_CORE), rows_mean, text_copies, copies_of(out_rows, owners)
+        window = key_windows(segment_ids)
+        return normed, take(normed, FROM_CORE), rows_mean, text_copies, copies_of(out_rows, owners), window
 
     shards, beside = gather_weights(own, first, second)
-    normed, other_normed, rows_mean, text_copies, out_copies = beside
+    normed, other_normed, rows_mean, text_copies, out_copies, window = beside
     own_out = lax.all_to_all(out_copies, "col", 0, 0, axis_index_groups=SAME_CORE)
-    for_other = attend(place, other_segs, other_normed, shards)
+    for_other = attend(place, key_windows(other_segs), other_segs, other_normed, shards)
     for_other, own_out = lax.optimization_barrier((for_other, own_out))
     context_other = take(for_other, FROM_CORE)
     own_out = own_out.reshape(width // 2, width)
     other_out = take(own_out, FROM_CORE)
     own_text = lax.all_to_all(text_copies, "col", 0, 0, axis_index_groups=SAME_CORE)
     own_text = own_text.reshape(owners, n_row, texts, width)
-    context_own = attend(place, segment_ids, normed, shards)
+    context_own = attend(place, window, segment_ids, normed, shards)
     unit, units = pool(rows_mean, context_own, context_other, own_out, other_out, n_row)
     units, own_text = lax.optimization_barrier((units, own_text))
     other_text = take(own_text, FROM_CORE)

time: 142 us -> 140 us (0.986)
  Pallas kernels: 70.7 us -> 68.2 us
  transfers between devices with their start and end apart: 20 -> 20, of which waited for: 6 -> 5; matrix products, arithmetic and copies ran while one was open for 4% -> 4% of each run, Pallas kernels for 46% -> 46%
where the time goes in v4:
time: 140 us; the launch traced here: 139 us
  Pallas kernels  68.2 us (49%)
  starting transfers between devices  48.3 us (34%)
  waiting for transfers between devices  14.1 us (10%)
  other arithmetic  4.74 us (3%)
  local copies, waits for them, and re-layouts  2.4 us (2%)
    pallas_call x2, Pallas kernels, attend(): pl.pallas_call(attend_kernel, grid=(1,), out_shape=jax.ShapeDtypeStruct((...  37.8 us
    ppermute x15, starting transfers between devices, take(): return lax.ppermute(values, AXES, found)  20.6 us
    ppermute x15, waiting for transfers between devices, take(): return lax.ppermute(values, AXES, found)  9.4 us
    all_to_all x1, starting transfers between devices, body(): terms = lax.all_to_all(terms.reshape(n_col, texts, width), 'col', 0, 0)  8.13 us
    pallas_call x1, Pallas kernels, encode(): pl.pallas_call(encode_kernel, grid=(count // rows,), out_shape=jax.ShapeD...  7.5 us
    all_to_all x1, starting transfers between devices, body(): lax.all_to_all(text_copies, 'col', 0, 0, axis_index_groups=SAME_CORE)  6.35 us
    pallas_call x3, Pallas kernels, copies_of(): pl.pallas_call(copies_kernel, grid=(1,), out_shape=jax.ShapeDtypeStruct(o...  5.59 us
    pallas_call x1, Pallas kernels, norm(): pl.pallas_call(norm_kernel, grid=(1,), out_shape=(jax.ShapeDtypeStruct((c...  5.48 us
  transfers between devices with their start and end apart: 20, of which 5 were waited for; matrix products, arithmetic and copies ran while one was open for 4% of the time, Pallas kernels for 46%

profile of v4, /device:TPU:1, one launch (start us, length us, event | category | flops | bytes accessed | tf_op | source)
XLA Modules:
  0.0 138.9 jit_solution(17553929305226090929)
XLA Ops:
  1.4 2.3 %pack.1 = (bf16[72,1728]{1,0:T(8,128)(2,1)}, bf16[72,1728]{1,0:T(8,128)(2,1)}) custom-call(s32[12]{0:T(128)} %stack.61.place_ref, bf16[72,1152]{1,0:T(8,128)(2,1)} %q_ref.1, bf16[72,1152]{1,0:T(8,128)(2,1)} %k_ref.1, bf16[72,1152]{1,0:T(8,128)(2,1)} %v_ref.1), custom_call_target="tpu_custom_call" | custom-call | bytes 2097152 | tf_op jit(solution)/shard_map/pack/pallas_call | solution.py:79
  7.7 2.9 %collective-permute-start.2 = (bf16[144,1728]{1,0:T(8,128)(2,1)S(1)}, bf16[144,1728]{1,0:T(8,128)(2,1)S(1)}, u32[]{:S(2)}, u32[]{:S(2)}) collective-permute-start(bf16[144,1728]{1,0:T(8,128)(2,1)S(1)} %maximum_select_fusion.refs_0_), channel_id=1, source_target_pairs={{4,0},{5,1},{20,16},{21,17},{6,2},{7,3},{22,18},{23,19},{8,4},{9,5... | collective-permute-start | bytes 1493000 | tf_op jit(solution)/shard_map/ppermute | solution.py:59
  10.6 3.8 %collective-permute-start.4 = (bf16[144,1728]{1,0:T(8,128)(2,1)S(1)}, bf16[144,1728]{1,0:T(8,128)(2,1)S(1)}, u32[]{:S(2)}, u32[]{:S(2)}) collective-permute-start(bf16[144,1728]{1,0:T(8,128)(2,1)S(1)} %maximum_select_fusion.refs_0_), channel_id=1, source_target_pairs={{18,0},{19,1},{2,16},{3,17},{16,2},{17,3},{0,18},{1,19},{22,4},{23... | collective-permute-start | bytes 1493000 | tf_op jit(solution)/shard_map/ppermute | solution.py:59
  15.8 4.2 %all-to-all-start = ((bf16[8,8,1152]{2,1,0:T(8,128)(2,1)}), bf16[8,8,1152]{2,1,0:T(8,128)(2,1)S(1)}, u32[]{:S(2)}, u32[]{:S(2)}) async-start(bf16[8,8,1152]{2,1,0:T(8,128)(2,1)} %copies.3), calls=%async_computation | async-start | bytes 294912 | tf_op jit(solution)/shard_map/all_to_all | solution.py:461
  20.5 5.5 %norm.1 = (bf16[1024,1280]{1,0:T(8,128)(2,1)}, f32[8,1152]{1,0:T(8,128)}) custom-call(bf16[1024,1152]{1,0:T(8,128)(2,1)} %x_ref.2, f32[1,1152]{1,0:T(1,128)} %reshape.256.gain_ref, s32[1,1024]{1,0:T(1,128)} %segs_ref.3), custom_call_target="tpu_custom_call" | custom-call | bytes 16777216 | tf_op jit(solution)/shard_map/norm/pallas_call | solution.py:131
  26.1 1.6 %collective-permute-start.8 = (bf16[1024,1280]{1,0:T(8,128)(2,1)}, bf16[1024,1280]{1,0:T(8,128)(2,1)}, u32[]{:S(2)}, u32[]{:S(2)}) collective-permute-start(bf16[1024,1280]{1,0:T(8,128)(2,1)} %get-tuple-element.52.normed_hbm), channel_id=1, source_target_pairs={{1,0},{0,1},{17,16},{16,17},{3,2},{2,3},{19,18},{18,19},{5,4},{4,5... | collective-permute-start | bytes 7864328 | tf_op jit(solution)/shard_map/ppermute | solution.py:59
  29.4 3.0 %collective-permute-start.5 = (bf16[144,1728]{1,0:T(8,128)(2,1)S(1)}, bf16[144,1728]{1,0:T(8,128)(2,1)S(1)}, u32[]{:S(2)}, u32[]{:S(2)}) collective-permute-start(bf16[144,1728]{1,0:T(8,128)(2,1)S(1)} %collective-permute-done.2.refs_1_), channel_id=1, source_target_pairs={{4,0},{5,1},{20,16},{21,17},{6,2},{7,3},{22,18},{23,19},{8,4},{9,5... | collective-permute-start | bytes 1493000 | tf_op jit(solution)/shard_map/ppermute | solution.py:59
  32.5 1.7 %collective-permute-start.6 = (bf16[144,1728]{1,0:T(8,128)(2,1)S(1)}, bf16[144,1728]{1,0:T(8,128)(2,1)S(1)}, u32[]{:S(2)}, u32[]{:S(2)}) collective-permute-start(bf16[144,1728]{1,0:T(8,128)(2,1)S(1)} %collective-permute-done.2.refs_1_), channel_id=1, source_target_pairs={{18,0},{19,1},{2,16},{3,17},{16,2},{17,3},{0,18},{1,19},{22,4},{23... | collective-permute-start | bytes 1493000 | tf_op jit(solution)/shard_map/ppermute | solution.py:59
  34.8 2.1 %copies.5 = bf16[8,72,1152]{2,1,0:T(8,128)(2,1)} custom-call(bf16[72,1152]{1,0:T(8,128)(2,1)} %in_ref.1), custom_call_target="tpu_custom_call" | custom-call | bytes 4194304 | tf_op jit(solution)/shard_map/copies/pallas_call | solution.py:97
  38.0 2.1 %copies.4 = bf16[8,64,1152]{2,1,0:T(8,128)(2,1)} custom-call(bf16[64,1152]{1,0:T(8,128)(2,1)} %bitcast.73), custom_call_target="tpu_custom_call" | custom-call | bytes 4194304 | tf_op jit(solution)/shard_map/copies/pallas_call | solution.py:97
  40.1 3.3 %collective-permute-done.5.refs_3_ = bf16[144,1728]{1,0:T(8,128)(2,1)S(1)} collective-permute-done((bf16[144,1728]{1,0:T(8,128)(2,1)S(1)}, bf16[144,1728]{1,0:T(8,128)(2,1)S(1)}, u32[]{:S(2)}, u32[]{:S(2)}) %collective-permute-start.5) | collective-permute-done | bytes 497696 | tf_op jit(solution)/shard_map/ppermute | solution.py:59
  43.5 3.1 %collective-permute-done.6.refs_5_ = bf16[144,1728]{1,0:T(8,128)(2,1)S(1)} collective-permute-done((bf16[144,1728]{1,0:T(8,128)(2,1)S(1)}, bf16[144,1728]{1,0:T(8,128)(2,1)S(1)}, u32[]{:S(2)}, u32[]{:S(2)}) %collective-permute-start.6) | collective-permute-done | bytes 497696 | tf_op jit(solution)/shard_map/ppermute | solution.py:59
  50.7 3.8 %all-to-all-start.1 = ((bf16[8,72,1152]{2,1,0:T(8,128)(2,1)}), bf16[8,72,1152]{2,1,0:T(8,128)(2,1)S(1)}, u32[]{:S(2)}, u32[]{:S(2)}) async-start(bf16[8,72,1152]{2,1,0:T(8,128)(2,1)} %copies.5), calls=%async_computation.1 | async-start | bytes 2654208 | tf_op jit(solution)/shard_map/all_to_all | solution.py:472
  55.1 18.9 %attend.3 = bf16[1040,640]{1,0:T(8,128)(2,1)} custom-call(s32[12]{0:T(128)} %stack.61.place_ref, s32[2,4]{1,0:T(2,128)} %pad_add_fusion.1.window_ref, s32[1,1024]{1,0:T(1,128)} %copy-done.10, bf16[1024,1280]{1,0:T(8,128)(2,1)} %collective-permute-done.8.normed_hbm, bf16[144,1728]{1,0:T(8,128)(2,1)} %copy-done.5, bf16[144,1728]{1,0:T(8,128)(2,1)} %copy-done.12, ...), custom_call_target="tpu_custom_call" | custom-call | flops 10000000000 | bytes 16777216 | tf_op jit(solution)/shard_map/attend/pallas_call | solution.py:261
  74.0 2.8 %collective-permute-start.12 = (bf16[1040,640]{1,0:T(8,128)(2,1)}, bf16[1040,640]{1,0:T(8,128)(2,1)}, u32[]{:S(2)}, u32[]{:S(2)}) collective-permute-start(bf16[1040,640]{1,0:T(8,128)(2,1)} %attend.3), channel_id=1, source_target_pairs={{1,0},{0,1},{17,16},{16,17},{3,2},{2,3},{19,18},{18,19},{5,4},{4,5... | collective-permute-start | bytes 3993608 | tf_op jit(solution)/shard_map/ppermute | solution.py:59
  76.9 6.3 %all-to-all-start.2 = ((bf16[8,64,1152]{2,1,0:T(8,128)(2,1)}), bf16[8,64,1152]{2,1,0:T(8,128)(2,1)S(1)}, u32[]{:S(2)}, u32[]{:S(2)}) async-start(bf16[8,64,1152]{2,1,0:T(8,128)(2,1)} %copies.4), calls=%async_computation.2 | async-start | bytes 2359296 | tf_op jit(solution)/shard_map/all_to_all | solution.py:478
  83.2 18.9 %attend.2.own_ref = bf16[1040,640]{1,0:T(8,128)(2,1)} custom-call(s32[12]{0:T(128)} %stack.61.place_ref, s32[2,4]{1,0:T(2,128)} %pad_add_fusion.window_ref, s32[1,1024]{1,0:T(1,128)} %segs_ref.3, bf16[1024,1280]{1,0:T(8,128)(2,1)} %get-tuple-element.52.normed_hbm, bf16[144,1728]{1,0:T(8,128)(2,1)} %copy-done.5, bf16[144,1728]{1,0:T(8,128)(2,1)} %copy-done.12, ...), custom_call_target="tpu_custom_call" | custom-call | flops 10000000000 | bytes 16777216 | tf_op jit(solution)/shard_map/attend/pallas_call | solution.py:261
  102.2 3.1 %pool.1 = (f32[8,1152]{1,0:T(8,128)}, bf16[8,8,1152]{2,1,0:T(8,128)(2,1)}) custom-call(f32[8,1152]{1,0:T(8,128)} %get-tuple-element.50.rows_mean_ref, bf16[1040,640]{1,0:T(8,128)(2,1)} %attend.2.own_ref, bf16[1040,640]{1,0:T(8,128)(2,1)} %collective-permute-done.12.other_ref, bf16[576,1152]{1,0:T(8,128)(2,1)} %bitcast.71, ...), custom_call_target="tpu_custom_call" | custom-call | flops 33554432 | bytes 4194304 | tf_op jit(solution)/shard_map/pool/pallas_call | solution.py:293
  106.0 5.3 %all-to-all-start.3 = ((bf16[8,8,1152]{2,1,0:T(8,128)(2,1)}), bf16[8,8,1152]{2,1,0:T(8,128)(2,1)S(1)}, u32[]{:S(2)}, u32[]{:S(2)}) async-start(bf16[8,8,1152]{2,1,0:T(8,128)(2,1)} %get-tuple-element.64), calls=%async_computation.3 | async-start | bytes 294912 | tf_op jit(solution)/shard_map/all_to_all | solution.py:484
  111.3 7.5 %encode.1 = bf16[1024,1152]{1,0:T(8,128)(2,1)} custom-call(bf16[1024,1152]{1,0:T(8,128)(2,1)} %x_ref.2, bf16[1040,640]{1,0:T(8,128)(2,1)} %attend.2.own_ref, bf16[1040,640]{1,0:T(8,128)(2,1)} %collective-permute-done.12.other_ref, bf16[576,1152]{1,0:T(8,128)(2,1)} %bitcast.72, bf16[576,1152]{1,0:T(8,128)(2,1)} %collective-permute-done.13.other_weight_ref), custom_call_target="tpu_custom_call" | custom-call | flops 3000000000 | bytes 16777216 | tf_op jit(solution)/shard_map/encode/pallas_call | solution.py:325
  118.8 2.0 %text_terms.1 = bf16[8,2,8,1152]{3,2,1,0:T(8,128)(2,1)} custom-call(s32[12]{0:T(128)S(1)} %copy-done.2, bf16[64,1152]{1,0:T(8,128)(2,1)S(1)} %bitcast.69, bf16[8,8,8,1152]{3,2,1,0:T(8,128)(2,1)S(1)} %bitcast.66, bf16[8,8,8,1152]{3,2,1,0:T(8,128)(2,1)S(1)} %collective-permute-done.14.theirs_ref), custom_call_target="tpu_custom_call" | custom-call | flops 67108864 | bytes 2097152 | tf_op jit(solution)/shard_map/text_terms/pallas_call | solution.py:369
  120.8 8.1 %all-to-all-start.4 = ((bf16[16,8,1152]{2,1,0:T(8,128)(2,1)}), bf16[16,8,1152]{2,1,0:T(8,128)(2,1)S(1)}, u32[]{:S(2)}, u32[]{:S(2)}) async-start(bf16[16,8,1152]{2,1,0:T(8,128)(2,1)} %bitcast.28), calls=%async_computation.4 | async-start | bytes 589824 | tf_op jit(solution)/shard_map/all_to_all | solution.py:489
  129.0 4.5 %image_gradient.1 = f32[8,1152]{1,0:T(8,128)} custom-call(s32[12]{0:T(128)} %stack.61.place_ref, f32[8,1152]{1,0:T(8,128)} %get-tuple-element.69.unit_ref, bf16[512,1152]{1,0:T(8,128)(2,1)} %bitcast.67, bf16[512,1152]{1,0:T(8,128)(2,1)} %bitcast.68), custom_call_target="tpu_custom_call" | custom-call | flops 268435456 | bytes 4194304 | tf_op jit(solution)/shard_map/image_gradient/pallas_call | solution.py:399
  133.5 4.7 %all-to-all-done.4 = bf16[16,8,1152]{2,1,0:T(8,128)(2,1)S(1)} async-done(((bf16[16,8,1152]{2,1,0:T(8,128)(2,1)}), bf16[16,8,1152]{2,1,0:T(8,128)(2,1)S(1)}, u32[]{:S(2)}, u32[]{:S(2)}) %all-to-all-start.4) | async-done | bytes 294944 | tf_op jit(solution)/shard_map/all_to_all | solution.py:489
  (81 shorter events, 16.3 us)
Async XLA Ops:
  0.6 19.3 %copy-start.11 = (f32[1152]{0:T(1024)S(1)}, f32[1152]{0:T(1024)}, u32[]{:S(2)}) copy-start(f32[1152]{0:T(1024)} %param.10) | copy-start | bytes 13828
  3.7 2.8 %collective-permute-start = (bf16[72,1728]{1,0:T(8,128)(2,1)}, bf16[72,1728]{1,0:T(8,128)(2,1)S(1)}, u32[]{:S(2)}, u32[]{:S(2)}) collective-permute-start(bf16[72,1728]{1,0:T(8,128)(2,1)} %get-tuple-element.38), channel_id=1, source_target_pairs={{1,0},{0,1},{17,16},{16,17},{3,2},{2,3},{19,18},{18,19},{5,4},{4,5... | collective-permute-start | bytes 746504 | tf_op jit(solution)/shard_map/ppermute | solution.py:59
  5.1 2.6 %collective-permute-start.1 = (s32[1,1024]{1,0:T(1,128)}, s32[1,1024]{1,0:T(1,128)S(1)}, u32[]{:S(2)}, u32[]{:S(2)}) collective-permute-start(s32[1,1024]{1,0:T(1,128)} %segs_ref.3), channel_id=1, source_target_pairs={{1,0},{0,1},{17,16},{16,17},{3,2},{2,3},{19,18},{18,19},{5,4},{4,5... | collective-permute-start | bytes 12296 | tf_op jit(solution)/shard_map/ppermute | solution.py:59
  7.7 18.3 %copy-start.5 = (bf16[144,1728]{1,0:T(8,128)(2,1)}, bf16[144,1728]{1,0:T(8,128)(2,1)S(1)}, u32[]{:S(2)}) copy-start(bf16[144,1728]{1,0:T(8,128)(2,1)S(1)} %maximum_select_fusion.refs_0_) | copy-start | bytes 1492996
  7.7 30.1 %copy-start.10 = (s32[1,1024]{1,0:T(1,128)}, s32[1,1024]{1,0:T(1,128)S(1)}, u32[]{:S(2)}) copy-start(s32[1,1024]{1,0:T(1,128)S(1)} %collective-permute-done.1.segs_ref) | copy-start | bytes 12292
  7.7 18.3 %collective-permute-start.2 = (bf16[144,1728]{1,0:T(8,128)(2,1)S(1)}, bf16[144,1728]{1,0:T(8,128)(2,1)S(1)}, u32[]{:S(2)}, u32[]{:S(2)}) collective-permute-start(bf16[144,1728]{1,0:T(8,128)(2,1)S(1)} %maximum_select_fusion.refs_0_), channel_id=1, source_target_pairs={{4,0},{5,1},{20,16},{21,17},{6,2},{7,3},{22,18},{23,19},{8,4},{9,5... | collective-permute-start | bytes 1493000 | tf_op jit(solution)/shard_map/ppermute | solution.py:59
  10.6 15.4 %collective-permute-start.3 = (bf16[144,1728]{1,0:T(8,128)(2,1)S(1)}, bf16[144,1728]{1,0:T(8,128)(2,1)S(1)}, u32[]{:S(2)}, u32[]{:S(2)}) collective-permute-start(bf16[144,1728]{1,0:T(8,128)(2,1)S(1)} %maximum_select_fusion.refs_0_), channel_id=1, source_target_pairs={{12,0},{13,1},{28,16},{29,17},{14,2},{15,3},{30,18},{31,19},{0,4},... | collective-permute-start | bytes 1493000 | tf_op jit(solution)/shard_map/ppermute | solution.py:59
  10.6 15.5 %collective-permute-start.4 = (bf16[144,1728]{1,0:T(8,128)(2,1)S(1)}, bf16[144,1728]{1,0:T(8,128)(2,1)S(1)}, u32[]{:S(2)}, u32[]{:S(2)}) collective-permute-start(bf16[144,1728]{1,0:T(8,128)(2,1)S(1)} %maximum_select_fusion.refs_0_), channel_id=1, source_target_pairs={{18,0},{19,1},{2,16},{3,17},{16,2},{17,3},{0,18},{1,19},{22,4},{23... | collective-permute-start | bytes 1493000 | tf_op jit(solution)/shard_map/ppermute | solution.py:59
  15.8 10.2 %all-to-all-start = ((bf16[8,8,1152]{2,1,0:T(8,128)(2,1)}), bf16[8,8,1152]{2,1,0:T(8,128)(2,1)S(1)}, u32[]{:S(2)}, u32[]{:S(2)}) async-start(bf16[8,8,1152]{2,1,0:T(8,128)(2,1)} %copies.3), calls=%async_computation | async-start | bytes 294912 | tf_op jit(solution)/shard_map/all_to_all | solution.py:461
  26.1 22.0 %collective-permute-start.8 = (bf16[1024,1280]{1,0:T(8,128)(2,1)}, bf16[1024,1280]{1,0:T(8,128)(2,1)}, u32[]{:S(2)}, u32[]{:S(2)}) collective-permute-start(bf16[1024,1280]{1,0:T(8,128)(2,1)} %get-tuple-element.52.normed_hbm), channel_id=1, source_target_pairs={{1,0},{0,1},{17,16},{16,17},{3,2},{2,3},{19,18},{18,19},{5,4},{4,5... | collective-permute-start | bytes 7864328 | tf_op jit(solution)/shard_map/ppermute | solution.py:59
  29.4 14.0 %collective-permute-start.5 = (bf16[144,1728]{1,0:T(8,128)(2,1)S(1)}, bf16[144,1728]{1,0:T(8,128)(2,1)S(1)}, u32[]{:S(2)}, u32[]{:S(2)}) collective-permute-start(bf16[144,1728]{1,0:T(8,128)(2,1)S(1)} %collective-permute-done.2.refs_1_), channel_id=1, source_target_pairs={{4,0},{5,1},{20,16},{21,17},{6,2},{7,3},{22,18},{23,19},{8,4},{9,5... | collective-permute-start | bytes 1493000 | tf_op jit(solution)/shard_map/ppermute | solution.py:59
  32.5 14.1 %collective-permute-start.6 = (bf16[144,1728]{1,0:T(8,128)(2,1)S(1)}, bf16[144,1728]{1,0:T(8,128)(2,1)S(1)}, u32[]{:S(2)}, u32[]{:S(2)}) collective-permute-start(bf16[144,1728]{1,0:T(8,128)(2,1)S(1)} %collective-permute-done.2.refs_1_), channel_id=1, source_target_pairs={{18,0},{19,1},{2,16},{3,17},{16,2},{17,3},{0,18},{1,19},{22,4},{23... | collective-permute-start | bytes 1493000 | tf_op jit(solution)/shard_map/ppermute | solution.py:59
  34.2 13.9 %collective-permute-start.7 = (bf16[144,1728]{1,0:T(8,128)(2,1)S(1)}, bf16[144,1728]{1,0:T(8,128)(2,1)S(1)}, u32[]{:S(2)}, u32[]{:S(2)}) collective-permute-start(bf16[144,1728]{1,0:T(8,128)(2,1)S(1)} %collective-permute-done.4.refs_4_), channel_id=1, source_target_pairs={{12,0},{13,1},{28,16},{29,17},{14,2},{15,3},{30,18},{31,19},{0,4},... | collective-permute-start | bytes 1493000 | tf_op jit(solution)/shard_map/ppermute | solution.py:59
  48.1 6.9 %collective-permute-start.9 = (bf16[48,1728]{1,0:T(8,128)(2,1)S(1)}, bf16[48,1728]{1,0:T(8,128)(2,1)}, u32[]{:S(2)}, u32[]{:S(2)}) collective-permute-start(bf16[48,1728]{1,0:T(8,128)(2,1)S(1)} %slice.23), channel_id=1, source_target_pairs={{18,0},{19,1},{2,16},{3,17},{16,2},{17,3},{0,18},{1,19},{22,4},{23... | collective-permute-start | bytes 497672 | tf_op jit(solution)/shard_map/ppermute | solution.py:59
  49.0 6.0 %collective-permute-start.10 = (bf16[48,1728]{1,0:T(8,128)(2,1)S(1)}, bf16[48,1728]{1,0:T(8,128)(2,1)}, u32[]{:S(2)}, u32[]{:S(2)}) collective-permute-start(bf16[48,1728]{1,0:T(8,128)(2,1)S(1)} %slice.24), channel_id=1, source_target_pairs={{4,0},{5,1},{20,16},{21,17},{6,2},{7,3},{22,18},{23,19},{8,4},{9,5... | collective-permute-start | bytes 497672 | tf_op jit(solution)/shard_map/ppermute | solution.py:59
  49.1 5.9 %collective-permute-start.11 = (bf16[48,1728]{1,0:T(8,128)(2,1)S(1)}, bf16[48,1728]{1,0:T(8,128)(2,1)}, u32[]{:S(2)}, u32[]{:S(2)}) collective-permute-start(bf16[48,1728]{1,0:T(8,128)(2,1)S(1)} %slice.25), channel_id=1, source_target_pairs={{12,0},{13,1},{28,16},{29,17},{14,2},{15,3},{30,18},{31,19},{0,4},... | collective-permute-start | bytes 497672 | tf_op jit(solution)/shard_map/ppermute | solution.py:59
  50.7 23.3 %all-to-all-start.1 = ((bf16[8,72,1152]{2,1,0:T(8,128)(2,1)}), bf16[8,72,1152]{2,1,0:T(8,128)(2,1)S(1)}, u32[]{:S(2)}, u32[]{:S(2)}) async-start(bf16[8,72,1152]{2,1,0:T(8,128)(2,1)} %copies.5), calls=%async_computation.1 | async-start | bytes 2654208 | tf_op jit(solution)/shard_map/all_to_all | solution.py:472
  74.0 28.2 %copy-start.3 = (bf16[8,72,1152]{2,1,0:T(8,128)(2,1)}, bf16[8,72,1152]{2,1,0:T(8,128)(2,1)S(1)}, u32[]{:S(2)}) copy-start(bf16[8,72,1152]{2,1,0:T(8,128)(2,1)S(1)} %all-to-all-done.1) | copy-start | bytes 3981316
  74.0 28.2 %collective-permute-start.12 = (bf16[1040,640]{1,0:T(8,128)(2,1)}, bf16[1040,640]{1,0:T(8,128)(2,1)}, u32[]{:S(2)}, u32[]{:S(2)}) collective-permute-start(bf16[1040,640]{1,0:T(8,128)(2,1)} %attend.3), channel_id=1, source_target_pairs={{1,0},{0,1},{17,16},{16,17},{3,2},{2,3},{19,18},{18,19},{5,4},{4,5... | collective-permute-start | bytes 3993608 | tf_op jit(solution)/shard_map/ppermute | solution.py:59
  76.8 25.4 %collective-permute-start.13 = (bf16[576,1152]{1,0:T(8,128)(2,1)S(1)}, bf16[576,1152]{1,0:T(8,128)(2,1)}, u32[]{:S(2)}, u32[]{:S(2)}) collective-permute-start(bf16[576,1152]{1,0:T(8,128)(2,1)S(1)} %bitcast.70), channel_id=1, source_target_pairs={{1,0},{0,1},{17,16},{16,17},{3,2},{2,3},{19,18},{18,19},{5,4},{4,5... | collective-permute-start | bytes 3981320 | tf_op jit(solution)/shard_map/ppermute | solution.py:59
  76.9 28.4 %all-to-all-start.2 = ((bf16[8,64,1152]{2,1,0:T(8,128)(2,1)}), bf16[8,64,1152]{2,1,0:T(8,128)(2,1)S(1)}, u32[]{:S(2)}, u32[]{:S(2)}) async-start(bf16[8,64,1152]{2,1,0:T(8,128)(2,1)} %copies.4), calls=%async_computation.2 | async-start | bytes 2359296 | tf_op jit(solution)/shard_map/all_to_all | solution.py:478
  105.3 13.5 %collective-permute-start.14 = (bf16[8,8,8,1152]{3,2,1,0:T(8,128)(2,1)S(1)}, bf16[8,8,8,1152]{3,2,1,0:T(8,128)(2,1)S(1)}, u32[]{:S(2)}, u32[]{:S(2)}) collective-permute-start(bf16[8,8,8,1152]{3,2,1,0:T(8,128)(2,1)S(1)} %bitcast.65), channel_id=1, source_target_pairs={{1,0},{0,1},{17,16},{16,17},{3,2},{2,3},{19,18},{18,19},{5,4},{4,5... | collective-permute-start | bytes 3538952 | tf_op jit(solution)/shard_map/ppermute | solution.py:59
  106.0 12.8 %all-to-all-start.3 = ((bf16[8,8,1152]{2,1,0:T(8,128)(2,1)}), bf16[8,8,1152]{2,1,0:T(8,128)(2,1)S(1)}, u32[]{:S(2)}, u32[]{:S(2)}) async-start(bf16[8,8,1152]{2,1,0:T(8,128)(2,1)} %get-tuple-element.64), calls=%async_computation.3 | async-start | bytes 294912 | tf_op jit(solution)/shard_map/all_to_all | solution.py:484
  120.8 17.3 %all-to-all-start.4 = ((bf16[16,8,1152]{2,1,0:T(8,128)(2,1)}), bf16[16,8,1152]{2,1,0:T(8,128)(2,1)S(1)}, u32[]{:S(2)}, u32[]{:S(2)}) async-start(bf16[16,8,1152]{2,1,0:T(8,128)(2,1)} %bitcast.28), calls=%async_computation.4 | async-start | bytes 589824 | tf_op jit(solution)/shard_map/all_to_all | solution.py:489
  (11 other events, 93.0 us)
